TPU v7x, 32 devices: a whole 2x2x4 slice. The times are simulated.
32 devices in a mesh: line: 8 (over y, x, core), batch: 4 (over z).
Axes of the slice: x: 2, y: 2, z: 4, core: 2. Of those that a mesh axis runs over, the one named last changes fastest.
Arguments:
- conserved: float32 [6, 192, 8, 1024], P(None, 'line', None, 'batch'), may hold values from -6 to 6
- flux_matrix: float32 [6, 6], replicated, may hold values from -2.5 to 2.5
- speed_xi: float32 [192, 8, 1024], P('line', None, 'batch'), may hold values from 0.2 to 2
- speed_eta: float32 [192, 8, 1024], P('line', None, 'batch'), may hold values from 0.2 to 2
- x_low1: float32 [192, 8, 1024], P('line', None, 'batch'), may hold values from -111 to -54
- x_low2: float32 [192, 8, 1024], P('line', None, 'batch'), may hold values from -1 to 1
- x_dinv: float32 [192, 8, 1024], P('line', None, 'batch'), may hold values from 0.009 to 0.018
- x_up1: float32 [192, 8, 1024], P('line', None, 'batch'), may hold values from -0.99 to -0.965
- x_up2: float32 [192, 8, 1024], P('line', None, 'batch'), may hold values from -0.008 to 0.008
- e_low1: float32 [192, 8, 1024], P('line', None, 'batch'), may hold values from -0.6 to -0.3
- e_low2: float32 [192, 8, 1024], P('line', None, 'batch'), may hold values from -0.2 to 0.2
- e_dinv: float32 [192, 8, 1024], P('line', None, 'batch'), may hold values from 0.6 to 0.9
- e_up1: float32 [192, 8, 1024], P('line', None, 'batch'), may hold values from -0.6 to -0.3
- e_up2: float32 [192, 8, 1024], P('line', None, 'batch'), may hold values from -0.2 to 0.2
- donor_index: int32 [8, 65536], P(None, ('line', 'batch')), may hold values from 0 to 32703
- donor_weight: float32 [8, 65536], P(None, ('line', 'batch')), may hold values from 0.05 to 0.25
- receive_index: int32 [65536], P(('line', 'batch')), may hold values from 0 to 49152, as said below
Outputs:
- updated: float32 [6, 192, 8, 1024], P(None, 'line', None, 'batch')
Inputs may be any that keep to these rules, and one draw needn't show every extreme that they name: `receive_index`: live cells of one device are distinct; the live slots of each pair of devices come first and the others hold 49152; some device receives all 64 slots from every device.
All inputs are finite; a program needn't handle non-finite values.
Results may differ from a plain program's by a relative error of at most 0.0001.
Values sent between devices are 32-bit elements; how exact they have to be, the bound alone decides.
No kernel may reach another device: no remote copies, remote signals or barrier semaphores. Data moves between devices by JAX's collectives and lax.ppermute only.
A program may use at most 192 MiB of HBM per device.

v0:
```python
import functools

import jax
import jax.numpy as jnp
from jax import lax
from jax.experimental import pallas as pl
from jax.experimental.pallas import tpu as pltpu
from jax.sharding import PartitionSpec as P

SUBITERS = 2
DISSIP = 0.02
STEP = 0.1

SUB = 8
LANES = 128
HALO = 2
SLOTS = 4

VM = pl.BlockSpec(memory_space=pltpu.VMEM)
SM = pl.BlockSpec(memory_space=pltpu.SMEM)
F32 = jnp.float32
I32 = jnp.int32


def f32(*shape):
    return jax.ShapeDtypeStruct(shape, F32)


class Sizes:
    def __init__(self, fields, cl, ne, lb):
        assert fields <= SUB and ne == SUB and lb % LANES == 0
        self.fields, self.cl, self.ne, self.lb = fields, cl, ne, lb
        self.halves = lb // LANES
        self.columns = self.halves * ne
        self.layer = self.columns * SUB
        self.rows = (cl + 2 * HALO) * self.layer
        assert lb & (lb - 1) == 0

    def at(self, i, h, j):
        return ((i * self.halves + h) * SUB + j) * SUB

    def row_of_cell(self, cell):
        k_bits = self.lb.bit_length() - 1
        half = (cell & (self.lb - 1)) >> 7
        j = (cell >> k_bits) & (SUB - 1)
        i = cell >> (k_bits + 3)
        return ((i + HALO) * self.halves + half) * (SUB * SUB) + j * SUB


def grid_of(axis):
    return lax.broadcasted_iota(I32, (SUB, LANES), axis)


def swap_corners(block):
    keep = (grid_of(0) < 4) == (grid_of(1) < LANES // 2)
    return jnp.where(keep, block, pltpu.roll(pltpu.roll(block, 4, 0), LANES // 2, 1))


def total(parts):
    parts = list(parts)
    while len(parts) > 1:
        parts = [parts[i] + parts[i + 1] if i + 1 < len(parts) else parts[i] for i in range(0, len(parts), 2)]
    return parts[0]


def gather_block(slots, block, donor, weight, tiles, out, picks):
    corners = donor.shape[0]
    lane = grid_of(1)
    down = lax.broadcasted_iota(I32, (LANES, LANES), 0)
    base = pl.multiple_of(block * LANES, LANES)
    for k in range(corners):
        cell = donor[k : k + 1, pl.ds(base, LANES)] & (LANES - 1)
        chosen = jnp.where(down == cell, weight[k : k + 1, pl.ds(base, LANES)], 0.0)
        picks[k * LANES : (k + 1) * LANES, :] = chosen.T
    result = jnp.zeros((SUB, LANES), F32)
    for n in range(LANES):
        parts = []
        for k in range(corners):
            row = pl.multiple_of(slots[k, n], SUB)
            parts.append(tiles[pl.ds(row, SUB), :] * picks[k * LANES + n : k * LANES + n + 1, :])
        result = jnp.where(lane == n, jnp.sum(total(parts), axis=1, keepdims=True), result)
    out[pl.ds(pl.multiple_of(block * SUB, SUB), SUB), :] = swap_corners(result)


def gather_all(z, donor, weight, tiles, out, picks, where, slots, sems):
    blocks = donor.shape[1] // LANES
    where[...] = z.row_of_cell(donor[...])

    def fetch(block, slot):
        source = where.at[:, pl.ds(pl.multiple_of(block * LANES, LANES), LANES)]
        return pltpu.make_async_copy(source, slots[slot], sems.at[slot])

    for slot in range(SLOTS):
        fetch(slot, slot).start()

    def lap(turn, carry):
        for slot in range(SLOTS):
            block = SLOTS * turn + slot
            fetch(block, slot).wait()
            gather_block(slots[slot], block, donor, weight, tiles, out, picks)

            @pl.when(block + SLOTS < blocks)
            def _():
                fetch(block + SLOTS, slot).start()

        return carry

    lax.fori_loop(0, blocks // SLOTS, lap, 0)


def gather_scratch(corners, count):
    return [
        pltpu.VMEM((corners * LANES, LANES), F32),
        pltpu.VMEM((corners, count), I32),
        *[pltpu.SMEM((corners, LANES), I32) for _ in range(SLOTS)],
        pltpu.SemaphoreType.DMA((SLOTS,)),
    ]


def first_kernel(z, donor, weight, conserved, out, tiles_out, tiles, picks, where, *rest):
    slots, sems = rest[:SLOTS], rest[SLOTS]
    tiles[...] = jnp.zeros(tiles.shape, F32)
    for f in range(z.fields):
        for i in range(z.cl):
            for h in range(z.halves):
                block = conserved[f, i, :, h * LANES : (h + 1) * LANES]
                tiles[pl.ds(z.at(i + HALO, h, 0) + f, SUB, stride=SUB), :] = block
    gather_all(z, donor, weight, tiles, out, picks, where, slots, sems)
    tiles_out[...] = tiles[...]


def place_kernel(z, place, receive, inbound, tiles, out, same_chip, next_chip, row_v, lane_v, row_s, lane_s, sems):
    blocks = receive.shape[0]
    lane = grid_of(1)
    cell = receive[...]
    row_v[...] = z.row_of_cell(cell)
    lane_v[...] = cell & (LANES - 1)
    rows = pltpu.make_async_copy(row_v, row_s, sems.at[0])
    lanes = pltpu.make_async_copy(lane_v, lane_s, sems.at[1])
    rows.start()
    lanes.start()
    out[...] = tiles[...]
    rows.wait()
    lanes.wait()

    def lap(block, carry):
        values = swap_corners(inbound[pl.ds(pl.multiple_of(block * SUB, SUB), SUB), :])
        for n in range(LANES):
            row = pl.multiple_of(row_s[block, n], SUB)
            column = jnp.broadcast_to(values[:, n : n + 1], (SUB, LANES))
            pltpu.store(out.at[pl.ds(row, SUB), :], column, mask=lane == lane_s[block, n])
        return carry

    lax.fori_loop(0, blocks, lap, 0)
    core = place[1]
    low, high = HALO * z.layer, z.cl * z.layer
    same_chip[...] = out[pl.ds(pl.multiple_of(jnp.where(core == 0, high, low), SUB), HALO * z.layer), :]
    next_chip[...] = out[pl.ds(pl.multiple_of(jnp.where(core == 0, low, high), SUB), HALO * z.layer), :]


def line_of(ref, i, h, j):
    return ref[i, j : j + 1, h * LANES : (h + 1) * LANES]


def lower_at(z, rhs, low1, low2, dinv, keep, state, i, h, j):
    row = z.at(i, h, j)
    one, two = state
    new = line_of(dinv, i, h, j) * (
        rhs[row : row + SUB, :] - line_of(low1, i, h, j) * one - line_of(low2, i, h, j) * two
    )
    keep[row : row + SUB, :] = new
    return (new, one)


def upper_at(z, keep, up1, up2, state, i, h, j):
    row = z.at(i, h, j)
    one, two = state
    new = keep[row : row + SUB, :] - line_of(up1, i, h, j) * one - line_of(up2, i, h, j) * two
    return (new, one)


def segment_kernel(z, low1, low2, dinv, up1, up2, out):
    for h in range(z.halves):
        cut = slice(h * LANES, (h + 1) * LANES)
        zero, one = jnp.zeros((SUB, LANES), F32), jnp.ones((SUB, LANES), F32)
        planes = [None] * 12
        for unit in range(2):
            a, b = (one, zero) if unit == 0 else (zero, one)
            kept = []
            for i in range(z.cl):
                a, b = -dinv[i, :, cut] * (low1[i, :, cut] * a + low2[i, :, cut] * b), a
                kept.append(a)
            planes[unit], planes[2 + unit] = a, b
            a, b = zero, zero
            for i in reversed(range(z.cl)):
                a, b = kept[i] - up1[i, :, cut] * a - up2[i, :, cut] * b, a
            planes[4 + unit], planes[6 + unit] = a, b
            a, b = (one, zero) if unit == 0 else (zero, one)
            for i in reversed(range(z.cl)):
                a, b = -up1[i, :, cut] * a - up2[i, :, cut] * b, a
            planes[8 + unit], planes[10 + unit] = a, b
        for p in range(12):
            row = p * z.columns + h * SUB
            out[row : row + SUB, :] = planes[p]


def residual_kernel(
    z, place, tiles, start, same_chip, next_chip, speed_xi, speed_eta, matrix,
    low1, low2, dinv, up1, up2, rhs, ends, field, slope, keep, spread,
):
    first = place[1] == 0
    edge = HALO * z.layer
    field[edge : edge + z.cl * z.layer, :] = tiles[edge : edge + z.cl * z.layer, :]
    field[0:edge, :] = jnp.where(first, next_chip[...], same_chip[...])
    field[z.rows - edge : z.rows, :] = jnp.where(first, same_chip[...], next_chip[...])
    columns = [jnp.broadcast_to(matrix[:, d : d + 1] * (-0.5 * STEP), (SUB, LANES)) for d in range(z.fields)]
    nothing = jnp.zeros((SUB, LANES), F32)

    def layer(i, carry):
        base = pl.multiple_of((i + HALO) * z.layer, SUB)

        def point(step, h, j):
            if j < 0 or j >= SUB:
                return nothing
            return field[pl.ds(base + step * z.layer + z.at(0, h, j), SUB), :]

        for h in range(z.halves):
            for j in range(SUB):
                row = z.at(0, h, j)
                centre = point(0, h, j)
                before, after = point(-1, h, j), point(1, h, j)
                under, over = point(0, h, j - 1), point(0, h, j + 1)
                change = line_of(speed_xi, i, h, j) * (after - before) + line_of(speed_eta, i, h, j) * (over - under)
                slope[row : row + SUB, :] = change
                near = (before + after) + (under + over)
                far = (point(-2, h, j) + point(2, h, j)) + (point(0, h, j - 2) + point(0, h, j + 2))
                fourth = far - 4.0 * near + 12.0 * centre
                value = -(STEP * DISSIP) * fourth - STEP * (centre - start[pl.ds(base + row, SUB), :])
                value = value + total(
                    [columns[d] * slope[row + d : row + d + 1, :] for d in range(z.fields)]
                )
                rhs[pl.ds(pl.multiple_of(i * z.layer, SUB) + row, SUB), :] = value
        return carry

    lax.fori_loop(0, z.cl, layer, 0)
    for h in range(z.halves):
        states = [(nothing, nothing)] * SUB
        for i in range(z.cl):
            states = [lower_at(z, rhs, low1, low2, dinv, keep, states[j], i, h, j) for j in range(SUB)]
        lowered = states
        states = [(nothing, nothing)] * SUB
        for i in reversed(range(z.cl)):
            states = [upper_at(z, keep, up1, up2, states[j], i, h, j) for j in range(SUB)]
        for j in range(SUB):
            for v, value in enumerate((*lowered[j], *states[j])):
                spread[pl.ds(v * z.columns + h * SUB + j, SUB, stride=4 * z.columns), :] = value
    ends[...] = spread[0 : z.fields * 4 * z.columns, :]


def solve_kernel(z, count, last, *refs):
    pairs = count // 2
    place, refs = refs[0], refs[1:]
    ends, maps, refs = refs[:count], refs[count : 2 * count], refs[2 * count :]
    (rhs, tiles, low1, low2, dinv, up1, up2, e_low1, e_low2, e_dinv, e_up1, e_up2), refs = refs[:12], refs[12:]
    if last:
        out, states, planes, spread, keep, fresh = refs
    else:
        donor, weight, out, tiles_out, states, planes, spread, keep, fresh, picks, where, *rest = refs
    me, core, chip = place[0], place[1], place[2]
    s_rows, m_rows = ends[0].shape[0], maps[0].shape[0]
    for s in range(pairs):
        for other in range(2):
            device = (chip ^ s) * 2 + (core ^ other)
            states[pl.ds(pl.multiple_of(device * s_rows, SUB), s_rows), :] = ends[2 * s + other][...]
            planes[pl.ds(pl.multiple_of(device * m_rows, SUB), m_rows), :] = maps[2 * s + other][...]

    zero = jnp.zeros((SUB, LANES), F32)
    for h in range(z.halves):

        def plane(device, p):
            row = device * m_rows + p * z.columns + h * SUB
            return planes[row : row + SUB, :]

        def end(device, f, v):
            row = device * s_rows + (f * 4 + v) * z.columns + h * SUB
            return states[row : row + SUB, :]

        entering = [[(zero, zero)] for _ in range(z.fields)]
        for d in range(count - 1):
            for f in range(z.fields):
                a, b = entering[f][-1]
                entering[f].append(
                    (
                        end(d, f, 0) + plane(d, 0) * a + plane(d, 1) * b,
                        end(d, f, 1) + plane(d, 2) * a + plane(d, 3) * b,
                    )
                )
        own = [[zero] * 4 for _ in range(z.fields)]
        returning = [(zero, zero)] * z.fields
        for d in reversed(range(count)):
            for f in range(z.fields):
                a, b = entering[f][d]
                g, k = returning[f]
                own[f] = [jnp.where(me == d, new, old) for new, old in zip((a, b, g, k), own[f])]
                returning[f] = (
                    (end(d, f, 2) + plane(d, 4) * a + plane(d, 5) * b) + (plane(d, 8) * g + plane(d, 9) * k),
                    (end(d, f, 3) + plane(d, 6) * a + plane(d, 7) * b) + (plane(d, 10) * g + plane(d, 11) * k),
                )
        for f in range(SUB):
            for v in range(4):
                row = (f * 4 + v) * z.columns + h * SUB
                spread[row : row + SUB, :] = own[f][v] if f < z.fields else zero

    def enter(v, h, j):
        return spread[pl.ds(v * z.columns + h * SUB + j, SUB, stride=4 * z.columns), :]

    if not last:
        fresh[0 : HALO * z.layer, :] = jnp.zeros((HALO * z.layer, LANES), F32)
        fresh[z.rows - HALO * z.layer : z.rows, :] = jnp.zeros((HALO * z.layer, LANES), F32)
    for h in range(z.halves):
        state = [(enter(0, h, j), enter(1, h, j)) for j in range(SUB)]
        for i in range(z.cl):
            state = [lower_at(z, rhs, low1, low2, dinv, keep, state[j], i, h, j) for j in range(SUB)]
        state = [(enter(2, h, j), enter(3, h, j)) for j in range(SUB)]
        for i in reversed(range(z.cl)):
            state = [upper_at(z, keep, up1, up2, state[j], i, h, j) for j in range(SUB)]
            one, two = zero, zero
            lowered = []
            for j in range(SUB):
                new = line_of(e_dinv, i, h, j) * (
                    state[j][0] - line_of(e_low1, i, h, j) * one - line_of(e_low2, i, h, j) * two
                )
                one, two = new, one
                lowered.append(new)
            one, two = zero, zero
            for j in reversed(range(SUB)):
                new = lowered[j] - line_of(e_up1, i, h, j) * one - line_of(e_up2, i, h, j) * two
                one, two = new, one
                row = z.at(i + HALO, h, j)
                fresh[row : row + SUB, :] = tiles[row : row + SUB, :] + new
    if last:
        for f in range(z.fields):
            for i in range(z.cl):
                for h in range(z.halves):
                    out[f, i, :, h * LANES : (h + 1) * LANES] = fresh[
                        pl.ds(z.at(i + HALO, h, 0) + f, SUB, stride=SUB), :
                    ]
    else:
        gather_all(z, donor, weight, fresh, out, picks, where, rest[:SLOTS], rest[SLOTS])
        tiles_out[...] = fresh[...]


def across_line(array):
    size = lax.axis_size("line")
    chips = size // 2
    result = []
    for s in range(chips):
        there = array
        if s:
            there = lax.ppermute(array, "line", [(i, i ^ (2 * s)) for i in range(size)])
        result.append(there)
        result.append(lax.ppermute(there, "line", [(i, i ^ 1) for i in range(size)]))
    return result


def local(
    conserved, flux_matrix, speed_xi, speed_eta, x_low1, x_low2, x_dinv, x_up1, x_up2,
    e_low1, e_low2, e_dinv, e_up1, e_up2, donor_index, donor_weight, receive_index,
):
    z = Sizes(*conserved.shape)
    count = lax.axis_size("line")
    devices = count * lax.axis_size("batch")
    corners, fringe = donor_index.shape
    assert fringe == devices * (LANES // 2) and count % 2 == 0 and count & (count - 1) == 0
    blocks = fringe // LANES
    me = lax.axis_index("line").astype(I32)
    place = jnp.stack([me, me & 1, me >> 1])
    matrix = jnp.pad(flux_matrix, ((0, SUB - z.fields), (0, LANES - z.fields)))
    receive = receive_index.reshape(blocks, LANES)
    x_coefs = (x_low1, x_low2, x_dinv, x_up1, x_up2)
    e_coefs = (e_low1, e_low2, e_dinv, e_up1, e_up2)
    params = pltpu.CompilerParams(vmem_limit_bytes=32 * 1024 * 1024)
    picked = f32(blocks * SUB, LANES)
    tile_shape = f32(z.rows, LANES)
    tile_mem = pltpu.VMEM((z.rows, LANES), F32)
    inner_mem = pltpu.VMEM((z.cl * z.layer, LANES), F32)
    spread_mem = pltpu.VMEM((SUB * 4 * z.columns, LANES), F32)
    s_rows, m_rows = z.fields * 4 * z.columns, 12 * z.columns

    maps = pl.pallas_call(
        functools.partial(segment_kernel, z),
        out_shape=f32(m_rows, LANES),
        in_specs=[VM] * 5,
        out_specs=VM,
        compiler_params=params,
        name="segments",
    )(*x_coefs)
    maps = across_line(maps)

    values, tiles = pl.pallas_call(
        functools.partial(first_kernel, z),
        out_shape=[picked, tile_shape],
        in_specs=[VM] * 3,
        out_specs=[VM] * 2,
        scratch_shapes=[tile_mem, *gather_scratch(corners, fringe)],
        compiler_params=params,
        name="donors",
    )(donor_index, donor_weight, conserved)
    start = tiles

    for sweep in range(SUBITERS):
        last = sweep == SUBITERS - 1
        inbound = lax.all_to_all(values.reshape(devices, 4, LANES), ("line", "batch"), 0, 0, tiled=True)
        inbound = inbound.reshape(blocks * SUB, LANES)
        tiles, same_chip, next_chip = pl.pallas_call(
            functools.partial(place_kernel, z),
            out_shape=[tile_shape, f32(HALO * z.layer, LANES), f32(HALO * z.layer, LANES)],
            in_specs=[SM] + [VM] * 3,
            out_specs=[VM] * 3,
            scratch_shapes=[
                pltpu.VMEM((blocks, LANES), I32),
                pltpu.VMEM((blocks, LANES), I32),
                pltpu.SMEM((blocks, LANES), I32),
                pltpu.SMEM((blocks, LANES), I32),
                pltpu.SemaphoreType.DMA((2,)),
            ],
            compiler_params=params,
            name="receivers",
        )(place, receive, inbound, tiles)
        same_chip = lax.ppermute(same_chip, "line", [(i, i ^ 1) for i in range(count)])
        facing = [(i, i + 1) for i in range(1, count - 1, 2)]
        next_chip = lax.ppermute(next_chip, "line", facing + [(b, a) for a, b in facing])
        rhs, ends = pl.pallas_call(
            functools.partial(residual_kernel, z),
            out_shape=[f32(z.cl * z.layer, LANES), f32(s_rows, LANES)],
            in_specs=[SM] + [VM] * 12,
            out_specs=[VM] * 2,
            scratch_shapes=[tile_mem, pltpu.VMEM((z.layer, LANES), F32), inner_mem, spread_mem],
            compiler_params=params,
            name="residual",
        )(place, tiles, start, same_chip, next_chip, speed_xi, speed_eta, matrix, *x_coefs)
        ends = across_line(ends)
        scratch = [
            pltpu.VMEM((count * s_rows, LANES), F32),
            pltpu.VMEM((count * m_rows, LANES), F32),
            spread_mem,
            inner_mem,
            tile_mem,
        ]
        operands = (place, *ends, *maps, rhs, tiles, *x_coefs, *e_coefs)
        if last:
            return pl.pallas_call(
                functools.partial(solve_kernel, z, count, True),
                out_shape=f32(*conserved.shape),
                in_specs=[SM] + [VM] * (len(operands) - 1),
                out_specs=VM,
                scratch_shapes=scratch,
                compiler_params=params,
                name="solve_last",
            )(*operands)
        operands = (*operands, donor_index, donor_weight)
        values, tiles = pl.pallas_call(
            functools.partial(solve_kernel, z, count, False),
            out_shape=[picked, tile_shape],
            in_specs=[SM] + [VM] * (len(operands) - 1),
            out_specs=[VM] * 2,
            scratch_shapes=[*scratch, *gather_scratch(corners, fringe)],
            compiler_params=params,
            name="solve_donors",
        )(*operands)


def solution(mesh):
    field = P(None, "line", None, "batch")
    coef = P("line", None, "batch")
    fringe = ("line", "batch")
    in_specs = (field, P(), *[coef] * 12, P(None, fringe), P(None, fringe), P(fringe))
    return jax.shard_map(local, mesh=mesh, in_specs=in_specs, out_specs=field, check_vma=False)
```

profile of v0, /device:TPU:0, one launch (start us, length us, event | category | flops | bytes accessed | tf_op | source)
XLA Modules:
  0.0 130.5 jit_solution(7761706392461591242)
XLA Ops:
  0.0 1.3 %copy-done.5 = f32[6,24,8,256]{3,2,1,0:T(8,128)S(1)} copy-done((f32[6,24,8,256]{3,2,1,0:T(8,128)S(1)}, f32[6,24,8,256]{3,2,1,0:T(8,128)}, u32[]{:S(2)}) %copy-start.5) | copy-done | bytes 1179672
  1.4 0.8 copy-done.13
  2.2 0.8 copy-done.15
  3.1 17.4 %donors.1 = (f32[128,128]{1,0:T(8,128)}, f32[3584,128]{1,0:T(8,128)S(1)}) custom-call(s32[8,2048]{1,0:T(8,128)S(1)} %copy-done.13, f32[8,2048]{1,0:T(8,128)S(1)} %copy-done.15, f32[6,24,8,256]{3,2,1,0:T(8,128)S(1)} %copy-done.5), custom_call_target="tpu_custom_call" | custom-call | tf_op jit(solution)/shard_map/donors/pallas_call | solution.py:400
  20.5 7.3 %all-to-all-start = ((f32[32,4,128]{2,1,0:T(4,128)}), f32[32,4,128]{2,1,0:T(4,128)S(1)}, u32[]{:S(2)}, u32[]{:S(2)}) async-start(f32[32,4,128]{2,1,0:T(4,128)} %bitcast.4), calls=%async_computation | async-start | bytes 131072 | tf_op jit(solution)/shard_map/all_to_all | solution.py:413
  27.9 7.4 %all-to-all-done = f32[32,4,128]{2,1,0:T(4,128)S(1)} async-done(((f32[32,4,128]{2,1,0:T(4,128)}), f32[32,4,128]{2,1,0:T(4,128)S(1)}, u32[]{:S(2)}, u32[]{:S(2)}) %all-to-all-start) | async-done | bytes 65568 | tf_op jit(solution)/shard_map/all_to_all | solution.py:413
  36.0 7.1 %receivers.2 = (f32[3584,128]{1,0:T(8,128)S(1)}, f32[256,128]{1,0:T(8,128)S(1)}, f32[256,128]{1,0:T(8,128)S(1)}) custom-call(s32[3]{0:T(128)S(1)} %pad_add_fusion.place.refs_0_, s32[16,128]{1,0:T(8,128)S(1)} %bitcast.11, f32[128,128]{1,0:T(8,128)S(1)} %bitcast.8, f32[3584,128]{1,0:T(8,128)S(1)} %get-tuple-element.20.tiles.start), custom_call_target="tpu_custom_call" | custom-call | tf_op jit(solution)/shard_map/receivers/pallas_call | solution.py:415
  43.2 0.8 collective-permute-start.1
  44.4 3.5 %collective-permute-start.14 = (f32[192,128]{1,0:T(8,128)S(1)}, f32[192,128]{1,0:T(8,128)S(1)}, u32[]{:S(2)}, u32[]{:S(2)}) collective-permute-start(f32[192,128]{1,0:T(8,128)S(1)} %segments.1.refs_9_), channel_id=1, source_target_pairs={{0,24},{4,28},{8,16},{12,20},{16,8},{20,12},{24,0},{28,4},{1,25},{... | collective-permute-start | bytes 294920 | tf_op jit(solution)/shard_map/ppermute | solution.py:360
  47.9 1.4 %collective-permute-start.12 = (f32[192,128]{1,0:T(8,128)S(1)}, f32[192,128]{1,0:T(8,128)S(1)}, u32[]{:S(2)}, u32[]{:S(2)}) collective-permute-start(f32[192,128]{1,0:T(8,128)S(1)} %segments.1.refs_9_), channel_id=1, source_target_pairs={{0,16},{4,20},{8,24},{12,28},{16,0},{20,4},{24,8},{28,12},{1,17},{... | collective-permute-start | bytes 294920 | tf_op jit(solution)/shard_map/ppermute | solution.py:360
  49.5 3.5 %residual.2 = (f32[3072,128]{1,0:T(8,128)S(1)}, f32[384,128]{1,0:T(8,128)S(1)}) custom-call(s32[3]{0:T(128)S(1)} %pad_add_fusion.place.refs_0_, f32[3584,128]{1,0:T(8,128)S(1)} %get-tuple-element.21.tiles.refs_18_, f32[3584,128]{1,0:T(8,128)S(1)} %get-tuple-element.20.tiles.start, f32[256,128]{1,0:T(8,128)S(1)} %collective-permute-done.same_chip, ...), custom_call_target="tpu_custom_call" | custom-call | tf_op jit(solution)/shard_map/residual/pallas_call | solution.py:433
  53.0 2.1 %collective-permute-start.7 = (f32[384,128]{1,0:T(8,128)S(1)}, f32[384,128]{1,0:T(8,128)S(1)}, u32[]{:S(2)}, u32[]{:S(2)}) collective-permute-start(f32[384,128]{1,0:T(8,128)S(1)} %get-tuple-element.24.refs_1_), channel_id=1, source_target_pairs={{0,24},{4,28},{8,16},{12,20},{16,8},{20,12},{24,0},{28,4},{1,25},{... | collective-permute-start | bytes 589832 | tf_op jit(solution)/shard_map/ppermute | solution.py:360
  55.1 1.4 %collective-permute-start.5 = (f32[384,128]{1,0:T(8,128)S(1)}, f32[384,128]{1,0:T(8,128)S(1)}, u32[]{:S(2)}, u32[]{:S(2)}) collective-permute-start(f32[384,128]{1,0:T(8,128)S(1)} %get-tuple-element.24.refs_1_), channel_id=1, source_target_pairs={{0,16},{4,20},{8,24},{12,28},{16,0},{20,4},{24,8},{28,12},{1,17},{... | collective-permute-start | bytes 589832 | tf_op jit(solution)/shard_map/ppermute | solution.py:360
  57.1 0.8 collective-permute-start.9
  58.0 0.9 collective-permute-done.9.refs_10_
  59.4 1.1 collective-permute-done.7.refs_7_
  60.5 2.4 %collective-permute-start.8 = (f32[384,128]{1,0:T(8,128)S(1)}, f32[384,128]{1,0:T(8,128)S(1)}, u32[]{:S(2)}, u32[]{:S(2)}) collective-permute-start(f32[384,128]{1,0:T(8,128)S(1)} %collective-permute-done.7.refs_7_), channel_id=1, source_target_pairs={{0,4},{4,0},{8,12},{12,8},{16,20},{20,16},{24,28},{28,24},{1,5},{5... | collective-permute-start | bytes 589832 | tf_op jit(solution)/shard_map/ppermute | solution.py:362
  62.9 3.0 %collective-permute-done.5.refs_5_ = f32[384,128]{1,0:T(8,128)S(1)} collective-permute-done((f32[384,128]{1,0:T(8,128)S(1)}, f32[384,128]{1,0:T(8,128)S(1)}, u32[]{:S(2)}, u32[]{:S(2)}) %collective-permute-start.5) | collective-permute-done | bytes 196640 | tf_op jit(solution)/shard_map/ppermute | solution.py:360
  66.5 1.3 collective-permute-done.11.refs_12_
  67.9 19.0 %solve_donors.1 = (f32[128,128]{1,0:T(8,128)S(1)}, f32[3584,128]{1,0:T(8,128)S(1)}) custom-call(s32[3]{0:T(128)S(1)} %pad_add_fusion.place.refs_0_, f32[384,128]{1,0:T(8,128)S(1)} %get-tuple-element.24.refs_1_, f32[384,128]{1,0:T(8,128)S(1)} %collective-permute-done.2.refs_2_, f32[384,128]{1,0:T(8,128)S(1)} %collective-permute-done.3.refs_3_, ...), custom_call_target="tpu_custom_call" | custom-call | tf_op jit(solution)/shard_map/solve_donors/pallas_call | solution.py:462
  86.9 9.6 %all_to_all.10 = f32[32,4,128]{2,1,0:T(4,128)S(1)} all-to-all(f32[32,4,128]{2,1,0:T(4,128)S(1)} %bitcast.10), channel_id=1, replica_groups=mesh['line'=8,'batch'=4] {'line','batch'}, dimensions={0} | all-to-all | bytes 131072 | tf_op jit(solution)/shard_map/all_to_all | solution.py:413
  96.5 7.1 %receivers.3 = (f32[3584,128]{1,0:T(8,128)S(1)}, f32[256,128]{1,0:T(8,128)S(1)}, f32[256,128]{1,0:T(8,128)S(1)}) custom-call(s32[3]{0:T(128)S(1)} %pad_add_fusion.place.refs_0_, s32[16,128]{1,0:T(8,128)S(1)} %bitcast.12, f32[128,128]{1,0:T(8,128)S(1)} %bitcast.9, f32[3584,128]{1,0:T(8,128)S(1)} %get-tuple-element.27.tiles), custom_call_target="tpu_custom_call" | custom-call | tf_op jit(solution)/shard_map/receivers/pallas_call | solution.py:415
  105.1 3.5 %residual.3 = (f32[3072,128]{1,0:T(8,128)S(1)}, f32[384,128]{1,0:T(8,128)S(1)}) custom-call(s32[3]{0:T(128)S(1)} %pad_add_fusion.place.refs_0_, f32[3584,128]{1,0:T(8,128)S(1)} %get-tuple-element.28.tiles.refs_18_, f32[3584,128]{1,0:T(8,128)S(1)} %get-tuple-element.20.tiles.start, f32[256,128]{1,0:T(8,128)S(1)} %collective-permute-done.16.same_chip, ...), custom_call_target="tpu_custom_call" | custom-call | tf_op jit(solution)/shard_map/residual/pallas_call | solution.py:433
  108.5 5.6 %collective-permute-start.23 = (f32[384,128]{1,0:T(8,128)S(1)}, f32[384,128]{1,0:T(8,128)S(1)}, u32[]{:S(2)}, u32[]{:S(2)}) collective-permute-start(f32[384,128]{1,0:T(8,128)S(1)} %get-tuple-element.31.refs_1_), channel_id=1, source_target_pairs={{0,24},{4,28},{8,16},{12,20},{16,8},{20,12},{24,0},{28,4},{1,25},{... | collective-permute-start | bytes 589832 | tf_op jit(solution)/shard_map/ppermute | solution.py:360
  114.2 1.9 %collective-permute-start.21 = (f32[384,128]{1,0:T(8,128)S(1)}, f32[384,128]{1,0:T(8,128)S(1)}, u32[]{:S(2)}, u32[]{:S(2)}) collective-permute-start(f32[384,128]{1,0:T(8,128)S(1)} %get-tuple-element.31.refs_1_), channel_id=1, source_target_pairs={{0,16},{4,20},{8,24},{12,28},{16,0},{20,4},{24,8},{28,12},{1,17},{... | collective-permute-start | bytes 589832 | tf_op jit(solution)/shard_map/ppermute | solution.py:360
  116.1 1.4 %collective-permute-start.19 = (f32[384,128]{1,0:T(8,128)S(1)}, f32[384,128]{1,0:T(8,128)S(1)}, u32[]{:S(2)}, u32[]{:S(2)}) collective-permute-start(f32[384,128]{1,0:T(8,128)S(1)} %get-tuple-element.31.refs_1_), channel_id=1, source_target_pairs={{0,8},{4,12},{8,0},{12,4},{16,24},{20,28},{24,16},{28,20},{1,9},{5... | collective-permute-start | bytes 589832 | tf_op jit(solution)/shard_map/ppermute | solution.py:360
  117.5 1.9 %collective-permute-done.23.refs_7_ = f32[384,128]{1,0:T(8,128)S(1)} collective-permute-done((f32[384,128]{1,0:T(8,128)S(1)}, f32[384,128]{1,0:T(8,128)S(1)}, u32[]{:S(2)}, u32[]{:S(2)}) %collective-permute-start.23) | collective-permute-done | bytes 196640 | tf_op jit(solution)/shard_map/ppermute | solution.py:360
  119.5 0.9 collective-permute-start.24
  120.4 4.0 %collective-permute-done.21.refs_5_ = f32[384,128]{1,0:T(8,128)S(1)} collective-permute-done((f32[384,128]{1,0:T(8,128)S(1)}, f32[384,128]{1,0:T(8,128)S(1)}, u32[]{:S(2)}, u32[]{:S(2)}) %collective-permute-start.21) | collective-permute-done | bytes 196640 | tf_op jit(solution)/shard_map/ppermute | solution.py:360
  124.5 0.9 collective-permute-done.19.refs_3_
  125.9 1.0 collective-permute-done.20.refs_4_
  126.9 3.6 %solve_last.1 = f32[6,24,8,256]{3,2,1,0:T(8,128)} custom-call(s32[3]{0:T(128)S(1)} %pad_add_fusion.place.refs_0_, f32[384,128]{1,0:T(8,128)S(1)} %get-tuple-element.31.refs_1_, f32[384,128]{1,0:T(8,128)S(1)} %collective-permute-done.18.refs_2_, f32[384,128]{1,0:T(8,128)S(1)} %collective-permute-done.19.refs_3_, ...), custom_call_target="tpu_custom_call" | custom-call | tf_op jit(solution)/shard_map/solve_last/pallas_call | solution.py:452
  (71 shorter events, 5.1 us)
Async XLA Ops:
  0.0 44.1 %copy-start.4 = (f32[24,8,256]{2,1,0:T(8,128)S(1)}, f32[24,8,256]{2,1,0:T(8,128)}, u32[]{:S(2)}) copy-start(f32[24,8,256]{2,1,0:T(8,128)} %refs_23_.3) | copy-start | bytes 589828
  0.0 44.1 %copy-start.3 = (f32[24,8,256]{2,1,0:T(8,128)S(1)}, f32[24,8,256]{2,1,0:T(8,128)}, u32[]{:S(2)}) copy-start(f32[24,8,256]{2,1,0:T(8,128)} %refs_22_.3) | copy-start | bytes 589828
  0.0 44.1 %copy-start.2 = (f32[24,8,256]{2,1,0:T(8,128)S(1)}, f32[24,8,256]{2,1,0:T(8,128)}, u32[]{:S(2)}) copy-start(f32[24,8,256]{2,1,0:T(8,128)} %refs_21_.3) | copy-start | bytes 589828
  0.0 44.1 %copy-start.1 = (f32[24,8,256]{2,1,0:T(8,128)S(1)}, f32[24,8,256]{2,1,0:T(8,128)}, u32[]{:S(2)}) copy-start(f32[24,8,256]{2,1,0:T(8,128)} %refs_20_.3) | copy-start | bytes 589828
  0.0 44.1 %copy-start = (f32[24,8,256]{2,1,0:T(8,128)S(1)}, f32[24,8,256]{2,1,0:T(8,128)}, u32[]{:S(2)}) copy-start(f32[24,8,256]{2,1,0:T(8,128)} %refs_19_.3) | copy-start | bytes 589828
  3.0 46.3 %copy-start.19 = (f32[6,6]{1,0:T(8,128)S(1)}, f32[6,6]{1,0:T(8,128)}, u32[]{:S(2)}) copy-start(f32[6,6]{1,0:T(8,128)} %param.18) | copy-start | bytes 436
  20.5 14.8 %all-to-all-start = ((f32[32,4,128]{2,1,0:T(4,128)}), f32[32,4,128]{2,1,0:T(4,128)S(1)}, u32[]{:S(2)}, u32[]{:S(2)}) async-start(f32[32,4,128]{2,1,0:T(4,128)} %bitcast.4), calls=%async_computation | async-start | bytes 131072 | tf_op jit(solution)/shard_map/all_to_all | solution.py:413
  43.2 6.2 %collective-permute-start = (f32[256,128]{1,0:T(8,128)S(1)}, f32[256,128]{1,0:T(8,128)S(1)}, u32[]{:S(2)}, u32[]{:S(2)}) collective-permute-start(f32[256,128]{1,0:T(8,128)S(1)} %get-tuple-element.22), channel_id=1, source_target_pairs={{0,4},{4,0},{8,12},{12,8},{16,20},{20,16},{24,28},{28,24},{1,5},{5... | collective-permute-start | bytes 393224 | tf_op jit(solution)/shard_map/ppermute | solution.py:430
  43.2 6.1 %collective-permute-start.1 = (f32[256,128]{1,0:T(8,128)S(1)}, f32[256,128]{1,0:T(8,128)S(1)}, u32[]{:S(2)}, u32[]{:S(2)}) collective-permute-start(f32[256,128]{1,0:T(8,128)S(1)} %get-tuple-element.23), channel_id=1, source_target_pairs={{4,8},{12,16},{20,24},{8,4},{16,12},{24,20},{5,9},{13,17},{21,25},... | collective-permute-start | bytes 393224 | tf_op jit(solution)/shard_map/ppermute | solution.py:432
  44.4 12.1 %collective-permute-start.14 = (f32[192,128]{1,0:T(8,128)S(1)}, f32[192,128]{1,0:T(8,128)S(1)}, u32[]{:S(2)}, u32[]{:S(2)}) collective-permute-start(f32[192,128]{1,0:T(8,128)S(1)} %segments.1.refs_9_), channel_id=1, source_target_pairs={{0,24},{4,28},{8,16},{12,20},{16,8},{20,12},{24,0},{28,4},{1,25},{... | collective-permute-start | bytes 294920 | tf_op jit(solution)/shard_map/ppermute | solution.py:360
  47.9 9.2 %collective-permute-start.12 = (f32[192,128]{1,0:T(8,128)S(1)}, f32[192,128]{1,0:T(8,128)S(1)}, u32[]{:S(2)}, u32[]{:S(2)}) collective-permute-start(f32[192,128]{1,0:T(8,128)S(1)} %segments.1.refs_9_), channel_id=1, source_target_pairs={{0,16},{4,20},{8,24},{12,28},{16,0},{20,4},{24,8},{28,12},{1,17},{... | collective-permute-start | bytes 294920 | tf_op jit(solution)/shard_map/ppermute | solution.py:360
  49.2 8.7 %collective-permute-start.10 = (f32[192,128]{1,0:T(8,128)S(1)}, f32[192,128]{1,0:T(8,128)S(1)}, u32[]{:S(2)}, u32[]{:S(2)}) collective-permute-start(f32[192,128]{1,0:T(8,128)S(1)} %segments.1.refs_9_), channel_id=1, source_target_pairs={{0,8},{4,12},{8,0},{12,4},{16,24},{20,28},{24,16},{28,20},{1,9},{5... | collective-permute-start | bytes 294920 | tf_op jit(solution)/shard_map/ppermute | solution.py:360
  53.0 7.5 %collective-permute-start.7 = (f32[384,128]{1,0:T(8,128)S(1)}, f32[384,128]{1,0:T(8,128)S(1)}, u32[]{:S(2)}, u32[]{:S(2)}) collective-permute-start(f32[384,128]{1,0:T(8,128)S(1)} %get-tuple-element.24.refs_1_), channel_id=1, source_target_pairs={{0,24},{4,28},{8,16},{12,20},{16,8},{20,12},{24,0},{28,4},{1,25},{... | collective-permute-start | bytes 589832 | tf_op jit(solution)/shard_map/ppermute | solution.py:360
  55.1 10.8 %collective-permute-start.5 = (f32[384,128]{1,0:T(8,128)S(1)}, f32[384,128]{1,0:T(8,128)S(1)}, u32[]{:S(2)}, u32[]{:S(2)}) collective-permute-start(f32[384,128]{1,0:T(8,128)S(1)} %get-tuple-element.24.refs_1_), channel_id=1, source_target_pairs={{0,16},{4,20},{8,24},{12,28},{16,0},{20,4},{24,8},{28,12},{1,17},{... | collective-permute-start | bytes 589832 | tf_op jit(solution)/shard_map/ppermute | solution.py:360
  56.4 9.5 %collective-permute-start.3 = (f32[384,128]{1,0:T(8,128)S(1)}, f32[384,128]{1,0:T(8,128)S(1)}, u32[]{:S(2)}, u32[]{:S(2)}) collective-permute-start(f32[384,128]{1,0:T(8,128)S(1)} %get-tuple-element.24.refs_1_), channel_id=1, source_target_pairs={{0,8},{4,12},{8,0},{12,4},{16,24},{20,28},{24,16},{28,20},{1,9},{5... | collective-permute-start | bytes 589832 | tf_op jit(solution)/shard_map/ppermute | solution.py:360
  57.1 1.8 %collective-permute-start.9 = (f32[192,128]{1,0:T(8,128)S(1)}, f32[192,128]{1,0:T(8,128)S(1)}, u32[]{:S(2)}, u32[]{:S(2)}) collective-permute-start(f32[192,128]{1,0:T(8,128)S(1)} %segments.1.refs_9_), channel_id=1, source_target_pairs={{0,4},{4,0},{8,12},{12,8},{16,20},{20,16},{24,28},{28,24},{1,5},{5... | collective-permute-start | bytes 294920 | tf_op jit(solution)/shard_map/ppermute | solution.py:362
  57.9 1.3 collective-permute-start.15
  58.9 7.6 %collective-permute-start.13 = (f32[192,128]{1,0:T(8,128)S(1)}, f32[192,128]{1,0:T(8,128)S(1)}, u32[]{:S(2)}, u32[]{:S(2)}) collective-permute-start(f32[192,128]{1,0:T(8,128)S(1)} %collective-permute-done.12.refs_13_), channel_id=1, source_target_pairs={{0,4},{4,0},{8,12},{12,8},{16,20},{20,16},{24,28},{28,24},{1,5},{5... | collective-permute-start | bytes 294920 | tf_op jit(solution)/shard_map/ppermute | solution.py:362
  59.2 8.5 %collective-permute-start.2 = (f32[384,128]{1,0:T(8,128)S(1)}, f32[384,128]{1,0:T(8,128)S(1)}, u32[]{:S(2)}, u32[]{:S(2)}) collective-permute-start(f32[384,128]{1,0:T(8,128)S(1)} %get-tuple-element.24.refs_1_), channel_id=1, source_target_pairs={{0,4},{4,0},{8,12},{12,8},{16,20},{20,16},{24,28},{28,24},{1,5},{5... | collective-permute-start | bytes 589832 | tf_op jit(solution)/shard_map/ppermute | solution.py:362
  60.5 7.3 %collective-permute-start.8 = (f32[384,128]{1,0:T(8,128)S(1)}, f32[384,128]{1,0:T(8,128)S(1)}, u32[]{:S(2)}, u32[]{:S(2)}) collective-permute-start(f32[384,128]{1,0:T(8,128)S(1)} %collective-permute-done.7.refs_7_), channel_id=1, source_target_pairs={{0,4},{4,0},{8,12},{12,8},{16,20},{20,16},{24,28},{28,24},{1,5},{5... | collective-permute-start | bytes 589832 | tf_op jit(solution)/shard_map/ppermute | solution.py:362
  65.9 1.9 %collective-permute-start.6 = (f32[384,128]{1,0:T(8,128)S(1)}, f32[384,128]{1,0:T(8,128)S(1)}, u32[]{:S(2)}, u32[]{:S(2)}) collective-permute-start(f32[384,128]{1,0:T(8,128)S(1)} %collective-permute-done.5.refs_5_), channel_id=1, source_target_pairs={{0,4},{4,0},{8,12},{12,8},{16,20},{20,16},{24,28},{28,24},{1,5},{5... | collective-permute-start | bytes 589832 | tf_op jit(solution)/shard_map/ppermute | solution.py:362
  66.0 1.8 %collective-permute-start.4 = (f32[384,128]{1,0:T(8,128)S(1)}, f32[384,128]{1,0:T(8,128)S(1)}, u32[]{:S(2)}, u32[]{:S(2)}) collective-permute-start(f32[384,128]{1,0:T(8,128)S(1)} %collective-permute-done.3.refs_3_), channel_id=1, source_target_pairs={{0,4},{4,0},{8,12},{12,8},{16,20},{20,16},{24,28},{28,24},{1,5},{5... | collective-permute-start | bytes 589832 | tf_op jit(solution)/shard_map/ppermute | solution.py:362
  66.4 1.3 %collective-permute-start.11 = (f32[192,128]{1,0:T(8,128)S(1)}, f32[192,128]{1,0:T(8,128)S(1)}, u32[]{:S(2)}, u32[]{:S(2)}) collective-permute-start(f32[192,128]{1,0:T(8,128)S(1)} %collective-permute-done.10.refs_11_), channel_id=1, source_target_pairs={{0,4},{4,0},{8,12},{12,8},{16,20},{20,16},{24,28},{28,24},{1,5},{5... | collective-permute-start | bytes 294920 | tf_op jit(solution)/shard_map/ppermute | solution.py:362
  103.6 1.4 %collective-permute-start.16 = (f32[256,128]{1,0:T(8,128)S(1)}, f32[256,128]{1,0:T(8,128)S(1)}, u32[]{:S(2)}, u32[]{:S(2)}) collective-permute-start(f32[256,128]{1,0:T(8,128)S(1)} %get-tuple-element.29), channel_id=1, source_target_pairs={{0,4},{4,0},{8,12},{12,8},{16,20},{20,16},{24,28},{28,24},{1,5},{5... | collective-permute-start | bytes 393224 | tf_op jit(solution)/shard_map/ppermute | solution.py:430
  103.7 1.3 %collective-permute-start.17 = (f32[256,128]{1,0:T(8,128)S(1)}, f32[256,128]{1,0:T(8,128)S(1)}, u32[]{:S(2)}, u32[]{:S(2)}) collective-permute-start(f32[256,128]{1,0:T(8,128)S(1)} %get-tuple-element.30), channel_id=1, source_target_pairs={{4,8},{12,16},{20,24},{8,4},{16,12},{24,20},{5,9},{13,17},{21,25},... | collective-permute-start | bytes 393224 | tf_op jit(solution)/shard_map/ppermute | solution.py:432
  108.5 10.9 %collective-permute-start.23 = (f32[384,128]{1,0:T(8,128)S(1)}, f32[384,128]{1,0:T(8,128)S(1)}, u32[]{:S(2)}, u32[]{:S(2)}) collective-permute-start(f32[384,128]{1,0:T(8,128)S(1)} %get-tuple-element.31.refs_1_), channel_id=1, source_target_pairs={{0,24},{4,28},{8,16},{12,20},{16,8},{20,12},{24,0},{28,4},{1,25},{... | collective-permute-start | bytes 589832 | tf_op jit(solution)/shard_map/ppermute | solution.py:360
  114.2 10.3 %collective-permute-start.21 = (f32[384,128]{1,0:T(8,128)S(1)}, f32[384,128]{1,0:T(8,128)S(1)}, u32[]{:S(2)}, u32[]{:S(2)}) collective-permute-start(f32[384,128]{1,0:T(8,128)S(1)} %get-tuple-element.31.refs_1_), channel_id=1, source_target_pairs={{0,16},{4,20},{8,24},{12,28},{16,0},{20,4},{24,8},{28,12},{1,17},{... | collective-permute-start | bytes 589832 | tf_op jit(solution)/shard_map/ppermute | solution.py:360
  116.1 9.3 %collective-permute-start.19 = (f32[384,128]{1,0:T(8,128)S(1)}, f32[384,128]{1,0:T(8,128)S(1)}, u32[]{:S(2)}, u32[]{:S(2)}) collective-permute-start(f32[384,128]{1,0:T(8,128)S(1)} %get-tuple-element.31.refs_1_), channel_id=1, source_target_pairs={{0,8},{4,12},{8,0},{12,4},{16,24},{20,28},{24,16},{28,20},{1,9},{5... | collective-permute-start | bytes 589832 | tf_op jit(solution)/shard_map/ppermute | solution.py:360
  117.5 8.0 %collective-permute-start.18 = (f32[384,128]{1,0:T(8,128)S(1)}, f32[384,128]{1,0:T(8,128)S(1)}, u32[]{:S(2)}, u32[]{:S(2)}) collective-permute-start(f32[384,128]{1,0:T(8,128)S(1)} %get-tuple-element.31.refs_1_), channel_id=1, source_target_pairs={{0,4},{4,0},{8,12},{12,8},{16,20},{20,16},{24,28},{28,24},{1,5},{5... | collective-permute-start | bytes 589832 | tf_op jit(solution)/shard_map/ppermute | solution.py:362
  119.5 6.0 %collective-permute-start.24 = (f32[384,128]{1,0:T(8,128)S(1)}, f32[384,128]{1,0:T(8,128)S(1)}, u32[]{:S(2)}, u32[]{:S(2)}) collective-permute-start(f32[384,128]{1,0:T(8,128)S(1)} %collective-permute-done.23.refs_7_), channel_id=1, source_target_pairs={{0,4},{4,0},{8,12},{12,8},{16,20},{20,16},{24,28},{28,24},{1,5},{5... | collective-permute-start | bytes 589832 | tf_op jit(solution)/shard_map/ppermute | solution.py:362
  124.5 1.4 %collective-permute-start.22 = (f32[384,128]{1,0:T(8,128)S(1)}, f32[384,128]{1,0:T(8,128)S(1)}, u32[]{:S(2)}, u32[]{:S(2)}) collective-permute-start(f32[384,128]{1,0:T(8,128)S(1)} %collective-permute-done.21.refs_5_), channel_id=1, source_target_pairs={{0,4},{4,0},{8,12},{12,8},{16,20},{20,16},{24,28},{28,24},{1,5},{5... | collective-permute-start | bytes 589832 | tf_op jit(solution)/shard_map/ppermute | solution.py:362
  125.5 1.4 %collective-permute-start.20 = (f32[384,128]{1,0:T(8,128)S(1)}, f32[384,128]{1,0:T(8,128)S(1)}, u32[]{:S(2)}, u32[]{:S(2)}) collective-permute-start(f32[384,128]{1,0:T(8,128)S(1)} %collective-permute-done.19.refs_3_), channel_id=1, source_target_pairs={{0,4},{4,0},{8,12},{12,8},{16,20},{20,16},{24,28},{28,24},{1,5},{5... | collective-permute-start | bytes 589832 | tf_op jit(solution)/shard_map/ppermute | solution.py:362
  (14 other events, 219.0 us)
where the time goes:
time: 131 us
  Pallas kernels  61.5 us (47%)
  starting transfers between devices  32.5 us (25%)
  waiting for transfers between devices  22.7 us (17%)
  blocking collectives  9.58 us (7%)
  local copies, waits for them, and re-layouts  3.81 us (3%)
    pallas_call x1, Pallas kernels, local(): pl.pallas_call(functools.partial(solve_kernel, z, count, False), out_shap...  19 us
    ppermute x9, starting transfers between devices, across_line(): there = lax.ppermute(array, 'line', [(i, i ^ 2 * s) for i in range(size)])  18.1 us
    pallas_call x1, Pallas kernels, local(): pl.pallas_call(functools.partial(first_kernel, z), out_shape=[picked, til...  17.4 us
    pallas_call x2, Pallas kernels, local(): pl.pallas_call(functools.partial(place_kernel, z), out_shape=[tile_shape,...  14.3 us
    ppermute x9, waiting for transfers between devices, across_line(): there = lax.ppermute(array, 'line', [(i, i ^ 2 * s) for i in range(size)])  11 us
    all_to_all x1, blocking collectives, local(): lax.all_to_all(values.reshape(devices, 4, LANES), ('line', 'batch'), 0, 0...  9.58 us
    all_to_all x1, waiting for transfers between devices, local(): lax.all_to_all(values.reshape(devices, 4, LANES), ('line', 'batch'), 0, 0...  7.41 us
    all_to_all x1, starting transfers between devices, local(): lax.all_to_all(values.reshape(devices, 4, LANES), ('line', 'batch'), 0, 0...  7.3 us
  transfers between devices with their start and end apart: 26, of which 11 were waited for; matrix products, arithmetic and copies ran while one was open for 0% of the time, Pallas kernels for 3%

commit v1 on v0

v1 whole, which is shorter than its diff:
```python
import functools

import jax
import jax.numpy as jnp
from jax import lax
from jax.experimental import pallas as pl
from jax.experimental.pallas import tpu as pltpu
from jax.sharding import PartitionSpec as P

SUBITERS = 2
DISSIP = 0.02
STEP = 0.1

SUB = 8
LANES = 128
HALO = 2
SLOTS = 4
GROUP = 2
MAPS = 12

VM = pl.BlockSpec(memory_space=pltpu.VMEM)
SM = pl.BlockSpec(memory_space=pltpu.SMEM)
F32 = jnp.float32
I32 = jnp.int32


def f32(*shape):
    return jax.ShapeDtypeStruct(shape, F32)


class Sizes:
    def __init__(self, fields, cl, ne, lb):
        assert fields <= SUB and ne == SUB and lb % LANES == 0
        self.fields, self.cl, self.ne, self.lb = fields, cl, ne, lb
        self.halves = lb // LANES
        self.columns = self.halves * ne
        self.layer = self.columns * SUB
        self.rows = (cl + 2 * HALO) * self.layer
        assert lb & (lb - 1) == 0

    def at(self, i, h, j):
        return ((i * self.halves + h) * SUB + j) * SUB

    def row_of_cell(self, cell):
        k_bits = self.lb.bit_length() - 1
        half = (cell & (self.lb - 1)) >> 7
        j = (cell >> k_bits) & (SUB - 1)
        i = cell >> (k_bits + 3)
        return ((i + HALO) * self.halves + half) * (SUB * SUB) + j * SUB


def grid_of(axis):
    return lax.broadcasted_iota(I32, (SUB, LANES), axis)


def swap_corners(block):
    keep = (grid_of(0) < 4) == (grid_of(1) < LANES // 2)
    return jnp.where(keep, block, pltpu.roll(pltpu.roll(block, 4, 0), LANES // 2, 1))


def total(parts):
    parts = list(parts)
    while len(parts) > 1:
        parts = [parts[i] + parts[i + 1] if i + 1 < len(parts) else parts[i] for i in range(0, len(parts), 2)]
    return parts[0]


def build_picks(k, block, donor, weight, picks):
    down = lax.broadcasted_iota(I32, (LANES, LANES), 0)
    base = pl.multiple_of(block * LANES, LANES)
    cell = donor[k : k + 1, pl.ds(base, LANES)] & (LANES - 1)
    chosen = jnp.where(down == cell, weight[k : k + 1, pl.ds(base, LANES)], 0.0)
    picks[k * LANES : (k + 1) * LANES, :] = chosen.T


def gather_block(corners, slots, block, tiles, out, picks, build_next):
    lane = grid_of(1)
    group = LANES // corners
    result = []
    for n in range(LANES):
        if n % group == 0:
            build_next(n // group)
        parts = []
        for k in range(corners):
            row = pl.multiple_of(slots[k, n], SUB)
            parts.append(tiles[pl.ds(row, SUB), :] * picks[k * LANES + n : k * LANES + n + 1, :])
        value = jnp.sum(total(parts), axis=1, keepdims=True)
        if n % 4 == 0:
            result.append(jnp.zeros((SUB, LANES), F32))
        result[-1] = jnp.where(lane == n, value, result[-1])
    out[pl.ds(pl.multiple_of(block * SUB, SUB), SUB), :] = swap_corners(total(result))


def gather_all(z, donor, weight, tiles, out, picks, where, slots, sems):
    corners = donor.shape[0]
    blocks = donor.shape[1] // LANES
    where[...] = z.row_of_cell(donor[...])

    def fetch(block, slot):
        source = where.at[:, pl.ds(pl.multiple_of(block * LANES, LANES), LANES)]
        return pltpu.make_async_copy(source, slots[slot], sems.at[slot])

    for slot in range(SLOTS):
        fetch(slot, slot).start()
    for k in range(corners):
        build_picks(k, 0, donor, weight, picks[0])

    def lap(turn, carry):
        for begin in range(0, SLOTS, GROUP):
            group = range(begin, begin + GROUP)
            for slot in group:
                fetch(SLOTS * turn + slot, slot).wait()
            for slot in group:
                block = SLOTS * turn + slot
                following = jnp.minimum(block + 1, blocks - 1)

                def build_next(k):
                    build_picks(k, following, donor, weight, picks[(slot + 1) % 2])

                gather_block(corners, slots[slot], block, tiles, out, picks[slot % 2], build_next)

            @pl.when(SLOTS * (turn + 1) < blocks)
            def _():
                for slot in group:
                    fetch(SLOTS * (turn + 1) + slot, slot).start()

        return carry

    lax.fori_loop(0, blocks // SLOTS, lap, 0)


def gather_scratch(corners, count):
    return [
        pltpu.VMEM((corners * LANES, LANES), F32),
        pltpu.VMEM((corners * LANES, LANES), F32),
        pltpu.VMEM((corners, count), I32),
        *[pltpu.SMEM((corners, LANES), I32) for _ in range(SLOTS)],
        pltpu.SemaphoreType.DMA((SLOTS,)),
    ]


def first_kernel(z, donor, weight, conserved, out, tiles_out, tiles, picks, picks_b, where, *rest):
    slots, sems = rest[:SLOTS], rest[SLOTS]
    tiles[...] = jnp.zeros(tiles.shape, F32)
    for f in range(z.fields):
        for i in range(z.cl):
            for h in range(z.halves):
                block = conserved[f, i, :, h * LANES : (h + 1) * LANES]
                tiles[pl.ds(z.at(i + HALO, h, 0) + f, SUB, stride=SUB), :] = block
    gather_all(z, donor, weight, tiles, out, (picks, picks_b), where, slots, sems)
    tiles_out[...] = tiles[...]


def place_kernel(z, place, receive, inbound, tiles, out, same_chip, next_chip, where, chosen, *rest):
    slots, sems = rest[:SLOTS], rest[SLOTS]
    blocks = receive.shape[0]
    lane = grid_of(1)
    cell = receive[...]
    where[pl.ds(0, blocks, stride=SUB), :] = z.row_of_cell(cell)

    def fetch(block, slot):
        source = where.at[pl.ds(pl.multiple_of(block * SUB, SUB), SUB), :]
        return pltpu.make_async_copy(source, slots[slot], sems.at[slot])

    for slot in range(SLOTS):
        fetch(slot, slot).start()
    out[...] = tiles[...]

    def lap(turn, carry):
        for slot in range(SLOTS):
            block = SLOTS * turn + slot
            values = swap_corners(inbound[pl.ds(pl.multiple_of(block * SUB, SUB), SUB), :])
            fetch(block, slot).wait()
            cell = receive[pl.ds(block, 1), :] & (LANES - 1)
            chosen[...] = jnp.where(lax.broadcasted_iota(I32, (LANES, LANES), 0) == cell, 1.0, 0.0).T
            for n in range(LANES):
                row = pl.multiple_of(slots[slot][0, n], SUB)
                mask = jnp.broadcast_to(chosen[n : n + 1, :], (SUB, LANES)) > 0.5
                column = jnp.sum(jnp.where(lane == n, values, 0.0), axis=1, keepdims=True)
                column = jnp.broadcast_to(column, (SUB, LANES))
                pltpu.store(out.at[pl.ds(row, SUB), :], column, mask=mask)

            @pl.when(block + SLOTS < blocks)
            def _():
                fetch(block + SLOTS, slot).start()

        return carry

    lax.fori_loop(0, blocks // SLOTS, lap, 0)
    core = place[1]
    low, high = HALO * z.layer, z.cl * z.layer
    same_chip[...] = out[pl.ds(pl.multiple_of(jnp.where(core == 0, high, low), SUB), HALO * z.layer), :]
    next_chip[...] = out[pl.ds(pl.multiple_of(jnp.where(core == 0, low, high), SUB), HALO * z.layer), :]


def line_of(ref, i, h, j):
    return ref[i, j : j + 1, h * LANES : (h + 1) * LANES]


def lower_at(z, rhs, low1, low2, dinv, keep, state, i, h, j):
    row = z.at(i, h, j)
    one, two = state
    inner, outer = rhs
    if i < HALO:
        right = outer[row : row + SUB, :]
    elif i < z.cl - HALO:
        right = inner[row - HALO * z.layer : row - HALO * z.layer + SUB, :]
    else:
        skip = (z.cl - 2 * HALO) * z.layer
        right = outer[row - skip : row - skip + SUB, :]
    new = line_of(dinv, i, h, j) * (
        right - line_of(low1, i, h, j) * one - line_of(low2, i, h, j) * two
    )
    keep[row : row + SUB, :] = new
    return (new, one)


def upper_at(z, keep, up1, up2, state, i, h, j):
    row = z.at(i, h, j)
    one, two = state
    new = keep[row : row + SUB, :] - line_of(up1, i, h, j) * one - line_of(up2, i, h, j) * two
    return (new, one)


def segment_kernel(z, low1, low2, dinv, up1, up2, out):
    for h in range(z.halves):
        cut = slice(h * LANES, (h + 1) * LANES)
        zero, one = jnp.zeros((SUB, LANES), F32), jnp.ones((SUB, LANES), F32)
        planes = [None] * MAPS
        for unit in range(2):
            a, b = (one, zero) if unit == 0 else (zero, one)
            kept = []
            for i in range(z.cl):
                a, b = -dinv[i, :, cut] * (low1[i, :, cut] * a + low2[i, :, cut] * b), a
                kept.append(a)
            planes[unit], planes[2 + unit] = a, b
            a, b = zero, zero
            for i in reversed(range(z.cl)):
                a, b = kept[i] - up1[i, :, cut] * a - up2[i, :, cut] * b, a
            planes[4 + unit], planes[6 + unit] = a, b
            a, b = (one, zero) if unit == 0 else (zero, one)
            for i in reversed(range(z.cl)):
                a, b = -up1[i, :, cut] * a - up2[i, :, cut] * b, a
            planes[8 + unit], planes[10 + unit] = a, b
        for p in range(12):
            row = (h * MAPS + p) * SUB
            out[row : row + SUB, :] = planes[p]


def compose_kernel(z, with_maps, place, own, other, own_maps, other_maps, *outs):
    chip, half = outs[0], outs[-1]
    first = place[1] == 0

    def pick(left, mine, theirs, row):
        block = mine[row : row + SUB, :], theirs[row : row + SUB, :]
        return jnp.where(first == left, *block)

    for h in range(z.halves):
        l = [pick(True, own_maps, other_maps, (h * MAPS + p) * SUB) for p in range(MAPS)]
        r = [pick(False, own_maps, other_maps, (h * MAPS + p) * SUB) for p in range(MAPS)]
        for f in range(z.fields):
            rows = [((h * z.fields + f) * 4 + v) * SUB for v in range(4)]
            a, b, g, k = [pick(True, own, other, row) for row in rows]
            c, d, m, n = [pick(False, own, other, row) for row in rows]
            c = c + r[0] * a + r[1] * b
            d = d + r[2] * a + r[3] * b
            m = m + r[4] * a + r[5] * b
            n = n + r[6] * a + r[7] * b
            g = g + l[8] * m + l[9] * n
            k = k + l[10] * m + l[11] * n
            for row, value in zip(rows, (c, d, g, k)):
                chip[row : row + SUB, :] = value
        if with_maps:
            t = [r[4] * l[0] + r[5] * l[2], r[4] * l[1] + r[5] * l[3]]
            t += [r[6] * l[0] + r[7] * l[2], r[6] * l[1] + r[7] * l[3]]
            both = [
                r[0] * l[0] + r[1] * l[2],
                r[0] * l[1] + r[1] * l[3],
                r[2] * l[0] + r[3] * l[2],
                r[2] * l[1] + r[3] * l[3],
                l[4] + l[8] * t[0] + l[9] * t[2],
                l[5] + l[8] * t[1] + l[9] * t[3],
                l[6] + l[10] * t[0] + l[11] * t[2],
                l[7] + l[10] * t[1] + l[11] * t[3],
                l[8] * r[8] + l[9] * r[10],
                l[8] * r[9] + l[9] * r[11],
                l[10] * r[8] + l[11] * r[10],
                l[10] * r[9] + l[11] * r[11],
            ]
            for p in range(MAPS):
                row = (h * MAPS + p) * SUB
                outs[1][row : row + SUB, :] = both[p]
    ends, maps = z.fields * 4 * SUB, MAPS * SUB
    half[0:ends, :] = chip[pl.ds(pl.multiple_of(place[1] * ends, SUB), ends), :]
    if with_maps:
        half[ends : ends + maps, :] = outs[1][pl.ds(pl.multiple_of(place[1] * maps, SUB), maps), :]


def flux_columns(z, matrix):
    return [jnp.broadcast_to(matrix[:, d : d + 1] * (-0.5 * STEP), (SUB, LANES)) for d in range(z.fields)]


def residual_layer(z, i, field, at, start, speed_xi, speed_eta, columns, slope, rhs, to):
    nothing = jnp.zeros((SUB, LANES), F32)

    def point(step, h, j):
        if j < 0 or j >= SUB:
            return nothing
        return field[pl.ds(at + step * z.layer + z.at(0, h, j), SUB), :]

    for h in range(z.halves):
        for j in range(SUB):
            row = z.at(0, h, j)
            centre = point(0, h, j)
            before, after = point(-1, h, j), point(1, h, j)
            under, over = point(0, h, j - 1), point(0, h, j + 1)
            change = line_of(speed_xi, i, h, j) * (after - before) + line_of(speed_eta, i, h, j) * (over - under)
            slope[row : row + SUB, :] = change
            near = (before + after) + (under + over)
            far = (point(-2, h, j) + point(2, h, j)) + (point(0, h, j - 2) + point(0, h, j + 2))
            fourth = far - 4.0 * near + 12.0 * centre
            value = -(STEP * DISSIP) * fourth - STEP * (centre - start[pl.ds((i + HALO) * z.layer + row, SUB), :])
            value = value + total([columns[d] * slope[row + d : row + d + 1, :] for d in range(z.fields)])
            rhs[pl.ds(to + row, SUB), :] = value


def interior_kernel(z, tiles, start, speed_xi, speed_eta, matrix, rhs, slope):
    columns = flux_columns(z, matrix)

    def layer(n, carry):
        at = pl.multiple_of((n + 2 * HALO) * z.layer, SUB)
        to = pl.multiple_of(n * z.layer, SUB)
        residual_layer(z, n + HALO, tiles, at, start, speed_xi, speed_eta, columns, slope, rhs, to)
        return carry

    lax.fori_loop(0, z.cl - 2 * HALO, layer, 0)


def edges_kernel(
    z, place, tiles, start, same_chip, next_chip, speed_xi, speed_eta, matrix,
    low1, low2, dinv, up1, up2, inner, outer, ends, low, high, slope, keep, spread,
):
    first = place[1] == 0
    edge, wide = HALO * z.layer, 2 * HALO * z.layer
    low[0:edge, :] = jnp.where(first, next_chip[...], same_chip[...])
    low[edge : edge + wide, :] = tiles[edge : edge + wide, :]
    high[wide : wide + edge, :] = jnp.where(first, same_chip[...], next_chip[...])
    high[0:wide, :] = tiles[z.rows - edge - wide : z.rows - edge, :]
    columns = flux_columns(z, matrix)
    for n in range(HALO):
        at, to = (n + HALO) * z.layer, n * z.layer
        residual_layer(z, n, low, at, start, speed_xi, speed_eta, columns, slope, outer, to)
        i = z.cl - HALO + n
        residual_layer(z, i, high, at, start, speed_xi, speed_eta, columns, slope, outer, edge + to)
    nothing = jnp.zeros((SUB, LANES), F32)
    for h in range(z.halves):
        states = [(nothing, nothing)] * SUB
        for i in range(z.cl):
            states = [lower_at(z, (inner, outer), low1, low2, dinv, keep, states[j], i, h, j) for j in range(SUB)]
        lowered = states
        states = [(nothing, nothing)] * SUB
        for i in reversed(range(z.cl)):
            states = [upper_at(z, keep, up1, up2, states[j], i, h, j) for j in range(SUB)]
        for j in range(SUB):
            for v, value in enumerate((*lowered[j], *states[j])):
                spread[pl.ds((h * SUB * 4 + v) * SUB + j, SUB, stride=4 * SUB), :] = value
        size = z.fields * 4 * SUB
        ends[h * size : (h + 1) * size, :] = spread[h * SUB * 4 * SUB : h * SUB * 4 * SUB + size, :]


def solve_kernel(z, chips, last, *refs):
    place, refs = refs[0], refs[1:]
    own, other, own_maps, other_maps, chip_ends, chip_maps = refs[:6]
    far, far_maps, refs = refs[6 : 4 + 2 * chips], refs[4 + 2 * chips : 2 + 4 * chips], refs[2 + 4 * chips :]
    rhs, refs = refs[:2], refs[2:]
    (tiles, low1, low2, dinv, up1, up2, e_low1, e_low2, e_dinv, e_up1, e_up2), refs = refs[:11], refs[11:]
    if last:
        out, states, planes, spread, keep, fresh = refs
    else:
        donor, weight, out, tiles_out, states, planes, spread, keep, fresh, picks, picks_b, where, *rest = refs
    core, chip = place[1], place[2]
    first = core == 0
    s_rows, m_rows = z.fields * 4 * SUB, MAPS * SUB

    def put(ref, at_chip, half, rows, source, begin):
        at = (at_chip * z.halves + half) * rows
        ref[pl.ds(pl.multiple_of(at, SUB), rows), :] = source[begin : begin + rows, :]

    for half in range(z.halves):
        put(states, chip, half, s_rows, chip_ends, half * s_rows)
        put(planes, chip, half, m_rows, chip_maps, half * m_rows)
    for s in range(1, chips):
        for t in range(2):
            put(states, chip ^ s, core ^ t, s_rows, far[2 * (s - 1) + t], 0)
            put(planes, chip ^ s, core ^ t, m_rows, far_maps[2 * (s - 1) + t], s_rows)

    zero = jnp.zeros((SUB, LANES), F32)
    for h in range(z.halves):

        def plane(at, p):
            row = ((at * z.halves + h) * MAPS + p) * SUB
            return planes[row : row + SUB, :]

        def end(at, f, v):
            row = ((at * z.halves + h) * z.fields * 4 + f * 4 + v) * SUB
            return states[row : row + SUB, :]

        entering = [[(zero, zero)] for _ in range(z.fields)]
        for d in range(chips - 1):
            for f in range(z.fields):
                a, b = entering[f][-1]
                entering[f].append(
                    (
                        end(d, f, 0) + plane(d, 0) * a + plane(d, 1) * b,
                        end(d, f, 1) + plane(d, 2) * a + plane(d, 3) * b,
                    )
                )
        mine = [[zero] * 4 for _ in range(z.fields)]
        returning = [(zero, zero)] * z.fields
        for d in reversed(range(chips)):
            for f in range(z.fields):
                a, b = entering[f][d]
                g, k = returning[f]
                mine[f] = [jnp.where(chip == d, new, old) for new, old in zip((a, b, g, k), mine[f])]
                returning[f] = (
                    (end(d, f, 2) + plane(d, 4) * a + plane(d, 5) * b) + (plane(d, 8) * g + plane(d, 9) * k),
                    (end(d, f, 3) + plane(d, 6) * a + plane(d, 7) * b) + (plane(d, 10) * g + plane(d, 11) * k),
                )

        def pick(left, one, two, row):
            return jnp.where(first == left, one[row : row + SUB, :], two[row : row + SUB, :])

        l = [pick(True, own_maps, other_maps, (h * MAPS + p) * SUB) for p in range(4)]
        r = [pick(False, own_maps, other_maps, (h * MAPS + p) * SUB) for p in range(MAPS)]
        for f in range(SUB):
            at = h * SUB * 4 + f * 4
            if f < z.fields:
                a, b, g, k = mine[f]
                rows = [((h * z.fields + f) * 4 + v) * SUB for v in range(4)]
                c = pick(True, own, other, rows[0]) + l[0] * a + l[1] * b
                d = pick(True, own, other, rows[1]) + l[2] * a + l[3] * b
                m = (pick(False, own, other, rows[2]) + r[4] * c + r[5] * d) + (r[8] * g + r[9] * k)
                n = (pick(False, own, other, rows[3]) + r[6] * c + r[7] * d) + (r[10] * g + r[11] * k)
                values = [jnp.where(first, a, c), jnp.where(first, b, d), jnp.where(first, m, g), jnp.where(first, n, k)]
            else:
                values = [zero] * 4
            for v in range(4):
                spread[(at + v) * SUB : (at + v + 1) * SUB, :] = values[v]

    def enter(v, h, j):
        return spread[pl.ds((h * SUB * 4 + v) * SUB + j, SUB, stride=4 * SUB), :]

    if not last:
        fresh[0 : HALO * z.layer, :] = jnp.zeros((HALO * z.layer, LANES), F32)
        fresh[z.rows - HALO * z.layer : z.rows, :] = jnp.zeros((HALO * z.layer, LANES), F32)
    for h in range(z.halves):
        state = [(enter(0, h, j), enter(1, h, j)) for j in range(SUB)]
        for i in range(z.cl):
            state = [lower_at(z, rhs, low1, low2, dinv, keep, state[j], i, h, j) for j in range(SUB)]
        state = [(enter(2, h, j), enter(3, h, j)) for j in range(SUB)]
        for i in reversed(range(z.cl)):
            state = [upper_at(z, keep, up1, up2, state[j], i, h, j) for j in range(SUB)]
            one, two = zero, zero
            lowered = []
            for j in range(SUB):
                new = line_of(e_dinv, i, h, j) * (
                    state[j][0] - line_of(e_low1, i, h, j) * one - line_of(e_low2, i, h, j) * two
                )
                one, two = new, one
                lowered.append(new)
            one, two = zero, zero
            for j in reversed(range(SUB)):
                new = lowered[j] - line_of(e_up1, i, h, j) * one - line_of(e_up2, i, h, j) * two
                one, two = new, one
                row = z.at(i + HALO, h, j)
                fresh[row : row + SUB, :] = tiles[row : row + SUB, :] + new
    if last:
        for f in range(z.fields):
            for i in range(z.cl):
                for h in range(z.halves):
                    out[f, i, :, h * LANES : (h + 1) * LANES] = fresh[
                        pl.ds(z.at(i + HALO, h, 0) + f, SUB, stride=SUB), :
                    ]
    else:
        tiles_out[...] = fresh[...]
        gather_all(z, donor, weight, fresh, out, (picks, picks_b), where, rest[:SLOTS], rest[SLOTS])


def to_other_core(array):
    return lax.ppermute(array, "line", [(i, i ^ 1) for i in range(lax.axis_size("line"))])


def from_other_chips(array):
    size = lax.axis_size("line")
    result = []
    for s in range(1, size // 2):
        there = lax.ppermute(array, "line", [(i, i ^ (2 * s)) for i in range(size)])
        result += [there, to_other_core(there)]
    return result


def local(
    conserved, flux_matrix, speed_xi, speed_eta, x_low1, x_low2, x_dinv, x_up1, x_up2,
    e_low1, e_low2, e_dinv, e_up1, e_up2, donor_index, donor_weight, receive_index,
):
    z = Sizes(*conserved.shape)
    count = lax.axis_size("line")
    devices = count * lax.axis_size("batch")
    corners, fringe = donor_index.shape
    assert fringe == devices * (LANES // 2) and count % 2 == 0 and count & (count - 1) == 0
    blocks = fringe // LANES
    me = lax.axis_index("line").astype(I32)
    place = jnp.stack([me, me & 1, me >> 1])
    matrix = jnp.pad(flux_matrix, ((0, SUB - z.fields), (0, LANES - z.fields)))
    receive = receive_index.reshape(blocks, LANES)
    x_coefs = (x_low1, x_low2, x_dinv, x_up1, x_up2)
    e_coefs = (e_low1, e_low2, e_dinv, e_up1, e_up2)
    params = pltpu.CompilerParams(vmem_limit_bytes=32 * 1024 * 1024)
    picked = f32(blocks * SUB, LANES)
    tile_shape = f32(z.rows, LANES)
    tile_mem = pltpu.VMEM((z.rows, LANES), F32)
    inner_mem = pltpu.VMEM((z.cl * z.layer, LANES), F32)
    spread_mem = pltpu.VMEM((SUB * 4 * z.columns, LANES), F32)
    s_rows, m_rows = z.fields * 4 * SUB, MAPS * SUB
    chips = count // 2
    assert z.halves == 2

    maps = pl.pallas_call(
        functools.partial(segment_kernel, z),
        out_shape=f32(z.halves * m_rows, LANES),
        in_specs=[VM] * 5,
        out_specs=VM,
        compiler_params=params,
        name="segments",
    )(*x_coefs)
    other_maps = to_other_core(maps)

    values, tiles = pl.pallas_call(
        functools.partial(first_kernel, z),
        out_shape=[picked, tile_shape],
        in_specs=[VM] * 3,
        out_specs=[VM] * 2,
        scratch_shapes=[tile_mem, *gather_scratch(corners, fringe)],
        compiler_params=params,
        name="donors",
    )(donor_index, donor_weight, conserved)
    start = tiles

    for sweep in range(SUBITERS):
        last = sweep == SUBITERS - 1
        inbound = lax.all_to_all(values.reshape(devices, 4, LANES), ("line", "batch"), 0, 0, tiled=True)
        inbound = inbound.reshape(blocks * SUB, LANES)
        tiles, same_chip, next_chip = pl.pallas_call(
            functools.partial(place_kernel, z),
            out_shape=[tile_shape, f32(HALO * z.layer, LANES), f32(HALO * z.layer, LANES)],
            in_specs=[SM] + [VM] * 3,
            out_specs=[VM] * 3,
            scratch_shapes=[
                pltpu.VMEM((blocks * SUB, LANES), I32),
                pltpu.VMEM((LANES, LANES), F32),
                *[pltpu.SMEM((SUB, LANES), I32) for _ in range(SLOTS)],
                pltpu.SemaphoreType.DMA((SLOTS,)),
            ],
            compiler_params=params,
            name="receivers",
        )(place, receive, inbound, tiles)
        same_chip = lax.ppermute(same_chip, "line", [(i, i ^ 1) for i in range(count)])
        facing = [(i, i + 1) for i in range(1, count - 1, 2)]
        next_chip = lax.ppermute(next_chip, "line", facing + [(b, a) for a, b in facing])
        layers = z.cl - 2 * HALO
        inner = pl.pallas_call(
            functools.partial(interior_kernel, z),
            out_shape=f32(layers * z.layer, LANES),
            in_specs=[VM] * 5,
            out_specs=VM,
            scratch_shapes=[pltpu.VMEM((z.layer, LANES), F32)],
            compiler_params=params,
            cost_estimate=pl.CostEstimate(
                flops=layers * z.layer * LANES * 40, bytes_accessed=layers * z.layer * LANES * 16, transcendentals=0
            ),
            name="interior",
        )(tiles, start, speed_xi, speed_eta, matrix)
        outer, ends = pl.pallas_call(
            functools.partial(edges_kernel, z),
            out_shape=[f32(2 * HALO * z.layer, LANES), f32(z.halves * s_rows, LANES)],
            in_specs=[SM] + [VM] * 13,
            out_specs=[VM] * 2,
            scratch_shapes=[
                pltpu.VMEM((3 * HALO * z.layer, LANES), F32),
                pltpu.VMEM((3 * HALO * z.layer, LANES), F32),
                pltpu.VMEM((z.layer, LANES), F32),
                inner_mem,
                spread_mem,
            ],
            compiler_params=params,
            name="edges",
        )(place, tiles, start, same_chip, next_chip, speed_xi, speed_eta, matrix, *x_coefs, inner)
        other_ends = to_other_core(ends)
        with_maps = sweep == 0
        shapes = [f32(z.halves * s_rows, LANES)]
        if with_maps:
            shapes.append(f32(z.halves * m_rows, LANES))
        shapes.append(f32(s_rows + m_rows * with_maps, LANES))
        composed = pl.pallas_call(
            functools.partial(compose_kernel, z, with_maps),
            out_shape=shapes,
            in_specs=[SM] + [VM] * 4,
            out_specs=[VM] * len(shapes),
            compiler_params=params,
            name="compose",
        )(place, ends, other_ends, maps, other_maps)
        chip_ends, half = composed[0], composed[-1]
        far = from_other_chips(half)
        if with_maps:
            chip_maps, far_maps = composed[1], far
        scratch = [
            pltpu.VMEM((chips * z.halves * s_rows, LANES), F32),
            pltpu.VMEM((chips * z.halves * m_rows, LANES), F32),
            spread_mem,
            inner_mem,
            tile_mem,
        ]
        operands = (place, ends, other_ends, maps, other_maps, chip_ends, chip_maps, *far, *far_maps)
        operands = (*operands, inner, outer, tiles, *x_coefs, *e_coefs)
        if last:
            return pl.pallas_call(
                functools.partial(solve_kernel, z, chips, True),
                out_shape=f32(*conserved.shape),
                in_specs=[SM] + [VM] * (len(operands) - 1),
                out_specs=VM,
                scratch_shapes=scratch,
                compiler_params=params,
                name="solve_last",
            )(*operands)
        operands = (*operands, donor_index, donor_weight)
        values, tiles = pl.pallas_call(
            functools.partial(solve_kernel, z, chips, False),
            out_shape=[picked, tile_shape],
            in_specs=[SM] + [VM] * (len(operands) - 1),
            out_specs=[VM] * 2,
            scratch_shapes=[*scratch, *gather_scratch(corners, fringe)],
            compiler_params=params,
            name="solve_donors",
        )(*operands)


def solution(mesh):
    field = P(None, "line", None, "batch")
    coef = P("line", None, "batch")
    fringe = ("line", "batch")
    in_specs = (field, P(), *[coef] * 12, P(None, fringe), P(None, fringe), P(fringe))
    return jax.shard_map(local, mesh=mesh, in_specs=in_specs, out_specs=field, check_vma=False)
```

time: 131 us -> 117 us (0.89)
  Pallas kernels: 61.5 us -> 54 us
  starting transfers between devices: 32.5 us -> 25.9 us
    ppermute x21 -> x15, starting transfers between devices: 23.5 us -> 17.1 us  [the longest x9 10 us: to_other_core(): lax.ppermute(array, 'line', [(i, i ^ 1) for i in range(lax.axis_size('lin...]
    pallas_call x2, Pallas kernels: 14.3 us -> 10.9 us  [local(): pl.pallas_call(functools.partial(place_kernel, z), out_shape=[tile_shape,...]
    pallas_call x1, Pallas kernels: 17.4 us -> 15 us  [local(): pl.pallas_call(functools.partial(first_kernel, z), out_shape=[picked, til...]
    pallas_call x5 -> x9, Pallas kernels: 29.8 us -> 28.1 us  [the longest x1 16.3 us: local(): pl.pallas_call(functools.partial(solve_kernel, z, chips, False), out_shap...]
    ppermute x21 -> x15, waiting for transfers between devices: 14.6 us -> 16 us  [the longest x6 11 us: from_other_chips(): there = lax.ppermute(array, 'line', [(i, i ^ 2 * s) for i in range(size)])]
  transfers between devices with their start and end apart: 26 -> 20, of which waited for: 11 -> 13; matrix products, arithmetic and copies ran while one was open for 0% -> 0% of each run, Pallas kernels for 3% -> 3%
where the time goes in v1:
time: 117 us
  Pallas kernels  54 us (46%)
  starting transfers between devices  25.9 us (22%)
  waiting for transfers between devices  23.4 us (20%)
  blocking collectives  9.37 us (8%)
  local copies, waits for them, and re-layouts  3.79 us (3%)
    pallas_call x1, Pallas kernels, local(): pl.pallas_call(functools.partial(solve_kernel, z, chips, False), out_shap...  16.3 us
    pallas_call x1, Pallas kernels, local(): pl.pallas_call(functools.partial(first_kernel, z), out_shape=[picked, til...  15 us
    ppermute x6, waiting for transfers between devices, from_other_chips(): there = lax.ppermute(array, 'line', [(i, i ^ 2 * s) for i in range(size)])  11 us
    pallas_call x2, Pallas kernels, local(): pl.pallas_call(functools.partial(place_kernel, z), out_shape=[tile_shape,...  10.9 us
    ppermute x9, starting transfers between devices, to_other_core(): lax.ppermute(array, 'line', [(i, i ^ 1) for i in range(lax.axis_size('lin...  10 us
    all_to_all x1, blocking collectives, local(): lax.all_to_all(values.reshape(devices, 4, LANES), ('line', 'batch'), 0, 0...  9.37 us
    all_to_all x1, waiting for transfers between devices, local(): lax.all_to_all(values.reshape(devices, 4, LANES), ('line', 'batch'), 0, 0...  7.41 us
    all_to_all x1, starting transfers between devices, local(): lax.all_to_all(values.reshape(devices, 4, LANES), ('line', 'batch'), 0, 0...  7.3 us
  transfers between devices with their start and end apart: 20, of which 13 were waited for; matrix products, arithmetic and copies ran while one was open for 0% of the time, Pallas kernels for 3%

profile of v1, /device:TPU:0, one launch (start us, length us, event | category | flops | bytes accessed | tf_op | source)
XLA Modules:
  0.0 117.0 jit_solution(17457954039725412662)
XLA Ops:
  0.0 1.3 %copy-done.7 = f32[6,24,8,256]{3,2,1,0:T(8,128)S(1)} copy-done((f32[6,24,8,256]{3,2,1,0:T(8,128)S(1)}, f32[6,24,8,256]{3,2,1,0:T(8,128)}, u32[]{:S(2)}) %copy-start.7) | copy-done | bytes 1179672
  1.3 0.8 copy-done.13
  2.2 0.8 copy-done.15
  3.0 15.0 %donors.1 = (f32[128,128]{1,0:T(8,128)}, f32[3584,128]{1,0:T(8,128)S(1)}) custom-call(s32[8,2048]{1,0:T(8,128)S(1)} %copy-done.13, f32[8,2048]{1,0:T(8,128)S(1)} %copy-done.15, f32[6,24,8,256]{3,2,1,0:T(8,128)S(1)} %copy-done.7), custom_call_target="tpu_custom_call" | custom-call | tf_op jit(solution)/shard_map/donors/pallas_call | solution.py:538
  18.1 7.3 %all-to-all-start = ((f32[32,4,128]{2,1,0:T(4,128)}), f32[32,4,128]{2,1,0:T(4,128)S(1)}, u32[]{:S(2)}, u32[]{:S(2)}) async-start(f32[32,4,128]{2,1,0:T(4,128)} %bitcast.4), calls=%async_computation | async-start | bytes 131072 | tf_op jit(solution)/shard_map/all_to_all | solution.py:551
  25.5 7.4 %all-to-all-done = f32[32,4,128]{2,1,0:T(4,128)S(1)} async-done(((f32[32,4,128]{2,1,0:T(4,128)}), f32[32,4,128]{2,1,0:T(4,128)S(1)}, u32[]{:S(2)}, u32[]{:S(2)}) %all-to-all-start) | async-done | bytes 65568 | tf_op jit(solution)/shard_map/all_to_all | solution.py:551
  32.9 0.7 copy-done.17
  33.6 5.5 %receivers.2 = (f32[3584,128]{1,0:T(8,128)S(1)}, f32[256,128]{1,0:T(8,128)S(1)}, f32[256,128]{1,0:T(8,128)S(1)}) custom-call(s32[3]{0:T(128)S(1)} %pad_add_fusion.place.refs_0_, s32[16,128]{1,0:T(8,128)S(1)} %bitcast.11, f32[128,128]{1,0:T(8,128)S(1)} %bitcast.8, f32[3584,128]{1,0:T(8,128)S(1)} %get-tuple-element.25.tiles.start), custom_call_target="tpu_custom_call" | custom-call | tf_op jit(solution)/shard_map/receivers/pallas_call | solution.py:553
  39.1 0.7 collective-permute-start.1
  39.9 1.9 %interior.2.inner.refs_19_ = f32[2560,128]{1,0:T(8,128)S(1)} custom-call(f32[3584,128]{1,0:T(8,128)S(1)} %get-tuple-element.26.tiles.refs_21_, f32[3584,128]{1,0:T(8,128)S(1)} %get-tuple-element.25.tiles.start, f32[24,8,256]{2,1,0:T(8,128)S(1)} %copy-done.5, f32[24,8,256]{2,1,0:T(8,128)S(1)} %copy-done.6, f32[8,128]{1,0:T(8,128)S(1)} %pad.4.matrix), custom_call_target="tpu_custom_call" | custom-call | flops 13107200 | bytes 5242880 | tf_op jit(solution)/shard_map/interior/pallas_call | solution.py:571
  42.0 1.5 %edges.2 = (f32[512,128]{1,0:T(8,128)S(1)}, f32[384,128]{1,0:T(8,128)S(1)}) custom-call(s32[3]{0:T(128)S(1)} %pad_add_fusion.place.refs_0_, f32[3584,128]{1,0:T(8,128)S(1)} %get-tuple-element.26.tiles.refs_21_, f32[3584,128]{1,0:T(8,128)S(1)} %get-tuple-element.25.tiles.start, f32[256,128]{1,0:T(8,128)S(1)} %collective-permute-done.same_chip, ...), custom_call_target="tpu_custom_call" | custom-call | tf_op jit(solution)/shard_map/edges/pallas_call | solution.py:583
  43.5 4.9 %collective-permute-start.2 = (f32[384,128]{1,0:T(8,128)S(1)}, f32[384,128]{1,0:T(8,128)S(1)}, u32[]{:S(2)}, u32[]{:S(2)}) collective-permute-start(f32[384,128]{1,0:T(8,128)S(1)} %get-tuple-element.29.own.refs_1_), channel_id=1, source_target_pairs={{0,4},{4,0},{8,12},{12,8},{16,20},{20,16},{24,28},{28,24},{1,5},{5... | collective-permute-start | bytes 589832 | tf_op jit(solution)/shard_map/ppermute | solution.py:490
  48.7 1.3 %collective-permute-done.3.other_maps.refs_4_ = f32[192,128]{1,0:T(8,128)S(1)} collective-permute-done((f32[192,128]{1,0:T(8,128)S(1)}, f32[192,128]{1,0:T(8,128)S(1)}, u32[]{:S(2)}, u32[]{:S(2)}) %collective-permute-start.3) | collective-permute-done | bytes 98336 | tf_op jit(solution)/shard_map/ppermute | solution.py:490
  50.7 2.2 %collective-permute-start.6 = (f32[288,128]{1,0:T(8,128)S(1)}, f32[288,128]{1,0:T(8,128)S(1)}, u32[]{:S(2)}, u32[]{:S(2)}) collective-permute-start(f32[288,128]{1,0:T(8,128)S(1)} %get-tuple-element.32), channel_id=1, source_target_pairs={{0,16},{4,20},{8,24},{12,28},{16,0},{20,4},{24,8},{28,12},{1,17},{... | collective-permute-start | bytes 442376 | tf_op jit(solution)/shard_map/ppermute | solution.py:497
  52.8 1.3 %collective-permute-start.4 = (f32[288,128]{1,0:T(8,128)S(1)}, f32[288,128]{1,0:T(8,128)S(1)}, u32[]{:S(2)}, u32[]{:S(2)}) collective-permute-start(f32[288,128]{1,0:T(8,128)S(1)} %get-tuple-element.32), channel_id=1, source_target_pairs={{0,8},{4,12},{8,0},{12,4},{16,24},{20,28},{24,16},{28,20},{1,9},{5... | collective-permute-start | bytes 442376 | tf_op jit(solution)/shard_map/ppermute | solution.py:497
  54.1 4.1 %collective-permute-done.8.refs_11_.refs_17_ = f32[288,128]{1,0:T(8,128)S(1)} collective-permute-done((f32[288,128]{1,0:T(8,128)S(1)}, f32[288,128]{1,0:T(8,128)S(1)}, u32[]{:S(2)}, u32[]{:S(2)}) %collective-permute-start.8) | collective-permute-done | bytes 147488 | tf_op jit(solution)/shard_map/ppermute | solution.py:497
  58.3 1.6 %collective-permute-done.6.refs_9_.refs_15_ = f32[288,128]{1,0:T(8,128)S(1)} collective-permute-done((f32[288,128]{1,0:T(8,128)S(1)}, f32[288,128]{1,0:T(8,128)S(1)}, u32[]{:S(2)}, u32[]{:S(2)}) %collective-permute-start.6) | collective-permute-done | bytes 147488 | tf_op jit(solution)/shard_map/ppermute | solution.py:497
  59.9 0.8 collective-permute-done.4.refs_7_.refs_13_
  61.2 0.8 collective-permute-done.5.refs_8_.refs_14_
  62.1 16.3 %solve_donors.1 = (f32[128,128]{1,0:T(8,128)S(1)}, f32[3584,128]{1,0:T(8,128)S(1)}) custom-call(s32[3]{0:T(128)S(1)} %pad_add_fusion.place.refs_0_, f32[384,128]{1,0:T(8,128)S(1)} %get-tuple-element.29.own.refs_1_, f32[384,128]{1,0:T(8,128)S(1)} %collective-permute-done.2.other.refs_2_, f32[192,128]{1,0:T(8,128)S(1)} %segments.1.own_maps.refs_3_, ...), custom_call_target="tpu_custom_call" | custom-call | tf_op jit(solution)/shard_map/solve_donors/pallas_call | solution.py:636
  78.4 9.4 %all_to_all.10 = f32[32,4,128]{2,1,0:T(4,128)S(1)} all-to-all(f32[32,4,128]{2,1,0:T(4,128)S(1)} %bitcast.10), channel_id=1, replica_groups=mesh['line'=8,'batch'=4] {'line','batch'}, dimensions={0} | all-to-all | bytes 131072 | tf_op jit(solution)/shard_map/all_to_all | solution.py:551
  87.8 5.5 %receivers.3 = (f32[3584,128]{1,0:T(8,128)S(1)}, f32[256,128]{1,0:T(8,128)S(1)}, f32[256,128]{1,0:T(8,128)S(1)}) custom-call(s32[3]{0:T(128)S(1)} %pad_add_fusion.place.refs_0_, s32[16,128]{1,0:T(8,128)S(1)} %bitcast.12, f32[128,128]{1,0:T(8,128)S(1)} %bitcast.9, f32[3584,128]{1,0:T(8,128)S(1)} %get-tuple-element.35.tiles), custom_call_target="tpu_custom_call" | custom-call | tf_op jit(solution)/shard_map/receivers/pallas_call | solution.py:553
  94.0 1.9 %interior.3.inner.refs_19_ = f32[2560,128]{1,0:T(8,128)S(1)} custom-call(f32[3584,128]{1,0:T(8,128)S(1)} %get-tuple-element.36.tiles.refs_21_, f32[3584,128]{1,0:T(8,128)S(1)} %get-tuple-element.25.tiles.start, f32[24,8,256]{2,1,0:T(8,128)S(1)} %copy-done.5, f32[24,8,256]{2,1,0:T(8,128)S(1)} %copy-done.6, f32[8,128]{1,0:T(8,128)S(1)} %pad.4.matrix), custom_call_target="tpu_custom_call" | custom-call | flops 13107200 | bytes 5242880 | tf_op jit(solution)/shard_map/interior/pallas_call | solution.py:571
  96.0 1.6 %edges.3 = (f32[512,128]{1,0:T(8,128)S(1)}, f32[384,128]{1,0:T(8,128)S(1)}) custom-call(s32[3]{0:T(128)S(1)} %pad_add_fusion.place.refs_0_, f32[3584,128]{1,0:T(8,128)S(1)} %get-tuple-element.36.tiles.refs_21_, f32[3584,128]{1,0:T(8,128)S(1)} %get-tuple-element.25.tiles.start, f32[256,128]{1,0:T(8,128)S(1)} %collective-permute-done.10.same_chip, ...), custom_call_target="tpu_custom_call" | custom-call | tf_op jit(solution)/shard_map/edges/pallas_call | solution.py:583
  97.5 5.1 %collective-permute-start.12 = (f32[384,128]{1,0:T(8,128)S(1)}, f32[384,128]{1,0:T(8,128)S(1)}, u32[]{:S(2)}, u32[]{:S(2)}) collective-permute-start(f32[384,128]{1,0:T(8,128)S(1)} %get-tuple-element.39.own.refs_1_), channel_id=1, source_target_pairs={{0,4},{4,0},{8,12},{12,8},{16,20},{20,16},{24,28},{28,24},{1,5},{5... | collective-permute-start | bytes 589832 | tf_op jit(solution)/shard_map/ppermute | solution.py:490
  102.6 1.1 collective-permute-done.12.other.refs_2_
  104.4 2.2 %collective-permute-start.15 = (f32[192,128]{1,0:T(8,128)S(1)}, f32[192,128]{1,0:T(8,128)S(1)}, u32[]{:S(2)}, u32[]{:S(2)}) collective-permute-start(f32[192,128]{1,0:T(8,128)S(1)} %get-tuple-element.41), channel_id=1, source_target_pairs={{0,16},{4,20},{8,24},{12,28},{16,0},{20,4},{24,8},{28,12},{1,17},{... | collective-permute-start | bytes 294920 | tf_op jit(solution)/shard_map/ppermute | solution.py:497
  106.5 1.3 %collective-permute-start.13 = (f32[192,128]{1,0:T(8,128)S(1)}, f32[192,128]{1,0:T(8,128)S(1)}, u32[]{:S(2)}, u32[]{:S(2)}) collective-permute-start(f32[192,128]{1,0:T(8,128)S(1)} %get-tuple-element.41), channel_id=1, source_target_pairs={{0,8},{4,12},{8,0},{12,4},{16,24},{20,28},{24,16},{28,20},{1,9},{5... | collective-permute-start | bytes 294920 | tf_op jit(solution)/shard_map/ppermute | solution.py:497
  107.9 3.1 %collective-permute-done.17.refs_11_ = f32[192,128]{1,0:T(8,128)S(1)} collective-permute-done((f32[192,128]{1,0:T(8,128)S(1)}, f32[192,128]{1,0:T(8,128)S(1)}, u32[]{:S(2)}, u32[]{:S(2)}) %collective-permute-start.17) | collective-permute-done | bytes 98336 | tf_op jit(solution)/shard_map/ppermute | solution.py:497
  110.9 0.7 collective-permute-done.15.refs_9_
  112.3 0.7 collective-permute-done.16.refs_10_
  113.6 3.4 %solve_last.1 = f32[6,24,8,256]{3,2,1,0:T(8,128)} custom-call(s32[3]{0:T(128)S(1)} %pad_add_fusion.place.refs_0_, f32[384,128]{1,0:T(8,128)S(1)} %get-tuple-element.39.own.refs_1_, f32[384,128]{1,0:T(8,128)S(1)} %collective-permute-done.12.other.refs_2_, f32[192,128]{1,0:T(8,128)S(1)} %segments.1.own_maps.refs_3_, ...), custom_call_target="tpu_custom_call" | custom-call | tf_op jit(solution)/shard_map/solve_last/pallas_call | solution.py:626
  (63 shorter events, 4.5 us)
Async XLA Ops:
  0.0 39.8 %copy-start.6 = (f32[24,8,256]{2,1,0:T(8,128)S(1)}, f32[24,8,256]{2,1,0:T(8,128)}, u32[]{:S(2)}) copy-start(f32[24,8,256]{2,1,0:T(8,128)} %speed_eta.7) | copy-start | bytes 589828
  0.0 39.8 %copy-start.5 = (f32[24,8,256]{2,1,0:T(8,128)S(1)}, f32[24,8,256]{2,1,0:T(8,128)}, u32[]{:S(2)}) copy-start(f32[24,8,256]{2,1,0:T(8,128)} %speed_xi.7) | copy-start | bytes 589828
  3.0 36.8 %copy-start.19 = (f32[6,6]{1,0:T(8,128)S(1)}, f32[6,6]{1,0:T(8,128)}, u32[]{:S(2)}) copy-start(f32[6,6]{1,0:T(8,128)} %param.18) | copy-start | bytes 436
  18.1 14.8 %all-to-all-start = ((f32[32,4,128]{2,1,0:T(4,128)}), f32[32,4,128]{2,1,0:T(4,128)S(1)}, u32[]{:S(2)}, u32[]{:S(2)}) async-start(f32[32,4,128]{2,1,0:T(4,128)} %bitcast.4), calls=%async_computation | async-start | bytes 131072 | tf_op jit(solution)/shard_map/all_to_all | solution.py:551
  39.0 2.9 %collective-permute-start = (f32[256,128]{1,0:T(8,128)S(1)}, f32[256,128]{1,0:T(8,128)S(1)}, u32[]{:S(2)}, u32[]{:S(2)}) collective-permute-start(f32[256,128]{1,0:T(8,128)S(1)} %get-tuple-element.27), channel_id=1, source_target_pairs={{0,4},{4,0},{8,12},{12,8},{16,20},{20,16},{24,28},{28,24},{1,5},{5... | collective-permute-start | bytes 393224 | tf_op jit(solution)/shard_map/ppermute | solution.py:567
  39.1 2.8 %collective-permute-start.1 = (f32[256,128]{1,0:T(8,128)S(1)}, f32[256,128]{1,0:T(8,128)S(1)}, u32[]{:S(2)}, u32[]{:S(2)}) collective-permute-start(f32[256,128]{1,0:T(8,128)S(1)} %get-tuple-element.28), channel_id=1, source_target_pairs={{4,8},{12,16},{20,24},{8,4},{16,12},{24,20},{5,9},{13,17},{21,25},... | collective-permute-start | bytes 393224 | tf_op jit(solution)/shard_map/ppermute | solution.py:569
  39.8 2.1 %copy-start = (f32[24,8,256]{2,1,0:T(8,128)S(1)}, f32[24,8,256]{2,1,0:T(8,128)}, u32[]{:S(2)}) copy-start(f32[24,8,256]{2,1,0:T(8,128)} %refs_22_.3) | copy-start | bytes 589828
  41.8 20.3 %copy-start.8 = (f32[24,8,256]{2,1,0:T(8,128)S(1)}, f32[24,8,256]{2,1,0:T(8,128)}, u32[]{:S(2)}) copy-start(f32[24,8,256]{2,1,0:T(8,128)} %refs_27_.3) | copy-start | bytes 589828
  41.8 20.3 %copy-start.9 = (f32[24,8,256]{2,1,0:T(8,128)S(1)}, f32[24,8,256]{2,1,0:T(8,128)}, u32[]{:S(2)}) copy-start(f32[24,8,256]{2,1,0:T(8,128)} %refs_28_.3) | copy-start | bytes 589828
  41.8 20.3 %copy-start.10 = (f32[24,8,256]{2,1,0:T(8,128)S(1)}, f32[24,8,256]{2,1,0:T(8,128)}, u32[]{:S(2)}) copy-start(f32[24,8,256]{2,1,0:T(8,128)} %refs_29_.3) | copy-start | bytes 589828
  41.9 20.2 %copy-start.11 = (f32[24,8,256]{2,1,0:T(8,128)S(1)}, f32[24,8,256]{2,1,0:T(8,128)}, u32[]{:S(2)}) copy-start(f32[24,8,256]{2,1,0:T(8,128)} %refs_30_.3) | copy-start | bytes 589828
  41.9 20.2 %copy-start.12 = (f32[24,8,256]{2,1,0:T(8,128)S(1)}, f32[24,8,256]{2,1,0:T(8,128)}, u32[]{:S(2)}) copy-start(f32[24,8,256]{2,1,0:T(8,128)} %refs_31_.3) | copy-start | bytes 589828
  41.9 20.2 %copy-start.14 = (s32[8,2048]{1,0:T(8,128)S(1)}, s32[8,2048]{1,0:T(8,128)}, u32[]{:S(2)}) copy-start(s32[8,2048]{1,0:T(8,128)} %refs_32_.1) | copy-start | bytes 196612
  41.9 20.2 %copy-start.16 = (f32[8,2048]{1,0:T(8,128)S(1)}, f32[8,2048]{1,0:T(8,128)}, u32[]{:S(2)}) copy-start(f32[8,2048]{1,0:T(8,128)} %refs_33_.1) | copy-start | bytes 196612
  43.5 6.4 %collective-permute-start.2 = (f32[384,128]{1,0:T(8,128)S(1)}, f32[384,128]{1,0:T(8,128)S(1)}, u32[]{:S(2)}, u32[]{:S(2)}) collective-permute-start(f32[384,128]{1,0:T(8,128)S(1)} %get-tuple-element.29.own.refs_1_), channel_id=1, source_target_pairs={{0,4},{4,0},{8,12},{12,8},{16,20},{20,16},{24,28},{28,24},{1,5},{5... | collective-permute-start | bytes 589832 | tf_op jit(solution)/shard_map/ppermute | solution.py:490
  48.6 1.4 %collective-permute-start.3 = (f32[192,128]{1,0:T(8,128)S(1)}, f32[192,128]{1,0:T(8,128)S(1)}, u32[]{:S(2)}, u32[]{:S(2)}) collective-permute-start(f32[192,128]{1,0:T(8,128)S(1)} %segments.1.own_maps.refs_3_), channel_id=1, source_target_pairs={{0,4},{4,0},{8,12},{12,8},{16,20},{20,16},{24,28},{28,24},{1,5},{5... | collective-permute-start | bytes 294920 | tf_op jit(solution)/shard_map/ppermute | solution.py:490
  50.6 7.7 %collective-permute-start.8 = (f32[288,128]{1,0:T(8,128)S(1)}, f32[288,128]{1,0:T(8,128)S(1)}, u32[]{:S(2)}, u32[]{:S(2)}) collective-permute-start(f32[288,128]{1,0:T(8,128)S(1)} %get-tuple-element.32), channel_id=1, source_target_pairs={{0,24},{4,28},{8,16},{12,20},{16,8},{20,12},{24,0},{28,4},{1,25},{... | collective-permute-start | bytes 442376 | tf_op jit(solution)/shard_map/ppermute | solution.py:497
  50.7 9.2 %collective-permute-start.6 = (f32[288,128]{1,0:T(8,128)S(1)}, f32[288,128]{1,0:T(8,128)S(1)}, u32[]{:S(2)}, u32[]{:S(2)}) collective-permute-start(f32[288,128]{1,0:T(8,128)S(1)} %get-tuple-element.32), channel_id=1, source_target_pairs={{0,16},{4,20},{8,24},{12,28},{16,0},{20,4},{24,8},{28,12},{1,17},{... | collective-permute-start | bytes 442376 | tf_op jit(solution)/shard_map/ppermute | solution.py:497
  52.8 7.9 %collective-permute-start.4 = (f32[288,128]{1,0:T(8,128)S(1)}, f32[288,128]{1,0:T(8,128)S(1)}, u32[]{:S(2)}, u32[]{:S(2)}) collective-permute-start(f32[288,128]{1,0:T(8,128)S(1)} %get-tuple-element.32), channel_id=1, source_target_pairs={{0,8},{4,12},{8,0},{12,4},{16,24},{20,28},{24,16},{28,20},{1,9},{5... | collective-permute-start | bytes 442376 | tf_op jit(solution)/shard_map/ppermute | solution.py:497
  58.3 2.4 %collective-permute-start.9 = (f32[288,128]{1,0:T(8,128)S(1)}, f32[288,128]{1,0:T(8,128)S(1)}, u32[]{:S(2)}, u32[]{:S(2)}) collective-permute-start(f32[288,128]{1,0:T(8,128)S(1)} %collective-permute-done.8.refs_11_.refs_17_), channel_id=1, source_target_pairs={{0,4},{4,0},{8,12},{12,8},{16,20},{20,16},{24,28},{28,24},{1,5},{5... | collective-permute-start | bytes 442376 | tf_op jit(solution)/shard_map/ppermute | solution.py:490
  59.9 1.4 %collective-permute-start.7 = (f32[288,128]{1,0:T(8,128)S(1)}, f32[288,128]{1,0:T(8,128)S(1)}, u32[]{:S(2)}, u32[]{:S(2)}) collective-permute-start(f32[288,128]{1,0:T(8,128)S(1)} %collective-permute-done.6.refs_9_.refs_15_), channel_id=1, source_target_pairs={{0,4},{4,0},{8,12},{12,8},{16,20},{20,16},{24,28},{28,24},{1,5},{5... | collective-permute-start | bytes 442376 | tf_op jit(solution)/shard_map/ppermute | solution.py:490
  60.7 1.4 %collective-permute-start.5 = (f32[288,128]{1,0:T(8,128)S(1)}, f32[288,128]{1,0:T(8,128)S(1)}, u32[]{:S(2)}, u32[]{:S(2)}) collective-permute-start(f32[288,128]{1,0:T(8,128)S(1)} %collective-permute-done.4.refs_7_.refs_13_), channel_id=1, source_target_pairs={{0,4},{4,0},{8,12},{12,8},{16,20},{20,16},{24,28},{28,24},{1,5},{5... | collective-permute-start | bytes 442376 | tf_op jit(solution)/shard_map/ppermute | solution.py:490
  62.1 25.7 %copy-start.18 = (s32[2048]{0:T(1024)S(1)}, s32[2048]{0:T(1024)}, u32[]{:S(2)}) copy-start(s32[2048]{0:T(1024)} %param.33) | copy-start | bytes 24580
  93.3 2.7 %collective-permute-start.10 = (f32[256,128]{1,0:T(8,128)S(1)}, f32[256,128]{1,0:T(8,128)S(1)}, u32[]{:S(2)}, u32[]{:S(2)}) collective-permute-start(f32[256,128]{1,0:T(8,128)S(1)} %get-tuple-element.37), channel_id=1, source_target_pairs={{0,4},{4,0},{8,12},{12,8},{16,20},{20,16},{24,28},{28,24},{1,5},{5... | collective-permute-start | bytes 393224 | tf_op jit(solution)/shard_map/ppermute | solution.py:567
  93.3 2.6 %collective-permute-start.11 = (f32[256,128]{1,0:T(8,128)S(1)}, f32[256,128]{1,0:T(8,128)S(1)}, u32[]{:S(2)}, u32[]{:S(2)}) collective-permute-start(f32[256,128]{1,0:T(8,128)S(1)} %get-tuple-element.38), channel_id=1, source_target_pairs={{4,8},{12,16},{20,24},{8,4},{16,12},{24,20},{5,9},{13,17},{21,25},... | collective-permute-start | bytes 393224 | tf_op jit(solution)/shard_map/ppermute | solution.py:569
  97.5 6.1 %collective-permute-start.12 = (f32[384,128]{1,0:T(8,128)S(1)}, f32[384,128]{1,0:T(8,128)S(1)}, u32[]{:S(2)}, u32[]{:S(2)}) collective-permute-start(f32[384,128]{1,0:T(8,128)S(1)} %get-tuple-element.39.own.refs_1_), channel_id=1, source_target_pairs={{0,4},{4,0},{8,12},{12,8},{16,20},{20,16},{24,28},{28,24},{1,5},{5... | collective-permute-start | bytes 589832 | tf_op jit(solution)/shard_map/ppermute | solution.py:490
  104.3 6.6 %collective-permute-start.17 = (f32[192,128]{1,0:T(8,128)S(1)}, f32[192,128]{1,0:T(8,128)S(1)}, u32[]{:S(2)}, u32[]{:S(2)}) collective-permute-start(f32[192,128]{1,0:T(8,128)S(1)} %get-tuple-element.41), channel_id=1, source_target_pairs={{0,24},{4,28},{8,16},{12,20},{16,8},{20,12},{24,0},{28,4},{1,25},{... | collective-permute-start | bytes 294920 | tf_op jit(solution)/shard_map/ppermute | solution.py:497
  104.4 7.3 %collective-permute-start.15 = (f32[192,128]{1,0:T(8,128)S(1)}, f32[192,128]{1,0:T(8,128)S(1)}, u32[]{:S(2)}, u32[]{:S(2)}) collective-permute-start(f32[192,128]{1,0:T(8,128)S(1)} %get-tuple-element.41), channel_id=1, source_target_pairs={{0,16},{4,20},{8,24},{12,28},{16,0},{20,4},{24,8},{28,12},{1,17},{... | collective-permute-start | bytes 294920 | tf_op jit(solution)/shard_map/ppermute | solution.py:497
  106.5 5.8 %collective-permute-start.13 = (f32[192,128]{1,0:T(8,128)S(1)}, f32[192,128]{1,0:T(8,128)S(1)}, u32[]{:S(2)}, u32[]{:S(2)}) collective-permute-start(f32[192,128]{1,0:T(8,128)S(1)} %get-tuple-element.41), channel_id=1, source_target_pairs={{0,8},{4,12},{8,0},{12,4},{16,24},{20,28},{24,16},{28,20},{1,9},{5... | collective-permute-start | bytes 294920 | tf_op jit(solution)/shard_map/ppermute | solution.py:497
  110.9 1.4 %collective-permute-start.18 = (f32[192,128]{1,0:T(8,128)S(1)}, f32[192,128]{1,0:T(8,128)S(1)}, u32[]{:S(2)}, u32[]{:S(2)}) collective-permute-start(f32[192,128]{1,0:T(8,128)S(1)} %collective-permute-done.17.refs_11_), channel_id=1, source_target_pairs={{0,4},{4,0},{8,12},{12,8},{16,20},{20,16},{24,28},{28,24},{1,5},{5... | collective-permute-start | bytes 294920 | tf_op jit(solution)/shard_map/ppermute | solution.py:490
  111.7 1.3 %collective-permute-start.16 = (f32[192,128]{1,0:T(8,128)S(1)}, f32[192,128]{1,0:T(8,128)S(1)}, u32[]{:S(2)}, u32[]{:S(2)}) collective-permute-start(f32[192,128]{1,0:T(8,128)S(1)} %collective-permute-done.15.refs_9_), channel_id=1, source_target_pairs={{0,4},{4,0},{8,12},{12,8},{16,20},{20,16},{24,28},{28,24},{1,5},{5... | collective-permute-start | bytes 294920 | tf_op jit(solution)/shard_map/ppermute | solution.py:490
  112.3 1.3 %collective-permute-start.14 = (f32[192,128]{1,0:T(8,128)S(1)}, f32[192,128]{1,0:T(8,128)S(1)}, u32[]{:S(2)}, u32[]{:S(2)}) collective-permute-start(f32[192,128]{1,0:T(8,128)S(1)} %collective-permute-done.13.refs_7_), channel_id=1, source_target_pairs={{0,4},{4,0},{8,12},{12,8},{16,20},{20,16},{24,28},{28,24},{1,5},{5... | collective-permute-start | bytes 294920 | tf_op jit(solution)/shard_map/ppermute | solution.py:490
  (8 other events, 12.0 us)

commit v2 on v1

--- a/solution.py
+++ b/solution.py
@@ -157,6 +157,7 @@
     lane = grid_of(1)
     cell = receive[...]
     where[pl.ds(0, blocks, stride=SUB), :] = z.row_of_cell(cell)
+    where[pl.ds(1, blocks, stride=SUB), :] = (cell - lax.broadcasted_iota(I32, (blocks, LANES), 1)) & (LANES - 1)
 
     def fetch(block, slot):
         source = where.at[pl.ds(pl.multiple_of(block * SUB, SUB), SUB), :]
@@ -167,22 +168,29 @@
     out[...] = tiles[...]
 
     def lap(turn, carry):
-        for slot in range(SLOTS):
-            block = SLOTS * turn + slot
-            values = swap_corners(inbound[pl.ds(pl.multiple_of(block * SUB, SUB), SUB), :])
-            fetch(block, slot).wait()
-            cell = receive[pl.ds(block, 1), :] & (LANES - 1)
-            chosen[...] = jnp.where(lax.broadcasted_iota(I32, (LANES, LANES), 0) == cell, 1.0, 0.0).T
-            for n in range(LANES):
-                row = pl.multiple_of(slots[slot][0, n], SUB)
-                mask = jnp.broadcast_to(chosen[n : n + 1, :], (SUB, LANES)) > 0.5
-                column = jnp.sum(jnp.where(lane == n, values, 0.0), axis=1, keepdims=True)
-                column = jnp.broadcast_to(column, (SUB, LANES))
-                pltpu.store(out.at[pl.ds(row, SUB), :], column, mask=mask)
-
-            @pl.when(block + SLOTS < blocks)
+        for begin in range(0, SLOTS, GROUP):
+            group = range(begin, begin + GROUP)
+            for slot in group:
+                fetch(SLOTS * turn + slot, slot).wait()
+            for slot in group:
+                cell = receive[pl.ds(SLOTS * turn + slot, 1), :] & (LANES - 1)
+                down = lax.broadcasted_iota(I32, (LANES, LANES), 0)
+                chosen[slot * LANES : (slot + 1) * LANES, :] = jnp.where(down == cell, 1.0, 0.0).T
+            for slot in group:
+                at = pl.multiple_of((SLOTS * turn + slot) * SUB, SUB)
+                values = swap_corners(inbound[pl.ds(at, SUB), :])
+                for n in range(LANES):
+                    row = pl.multiple_of(slots[slot][0, n], SUB)
+                    pick = chosen[slot * LANES + n : slot * LANES + n + 1, :]
+                    mask = jnp.broadcast_to(pick, (SUB, LANES)) > 0.5
+                    column = jnp.sum(jnp.where(lane == n, values, 0.0), axis=1, keepdims=True)
+                    column = jnp.broadcast_to(column, (SUB, LANES))
+                    pltpu.store(out.at[pl.ds(row, SUB), :], column, mask=mask)
+
+            @pl.when(SLOTS * (turn + 1) < blocks)
             def _():
-                fetch(block + SLOTS, slot).start()
+                for slot in group:
+                    fetch(SLOTS * (turn + 1) + slot, slot).start()
 
         return carry
 
@@ -337,14 +345,15 @@
 
 
 def edges_kernel(
-    z, place, tiles, start, same_chip, next_chip, speed_xi, speed_eta, matrix,
+    z, line, place, tiles, start, same_chip, next_chip, speed_xi, speed_eta, matrix,
     low1, low2, dinv, up1, up2, inner, outer, ends, low, high, slope, keep, spread,
 ):
     first = place[1] == 0
     edge, wide = HALO * z.layer, 2 * HALO * z.layer
-    low[0:edge, :] = jnp.where(first, next_chip[...], same_chip[...])
+    low[0:edge, :] = jnp.where(place[0] == 0, 0.0, jnp.where(first, next_chip[...], same_chip[...]))
     low[edge : edge + wide, :] = tiles[edge : edge + wide, :]
-    high[wide : wide + edge, :] = jnp.where(first, same_chip[...], next_chip[...])
+    after = jnp.where(first, same_chip[...], next_chip[...])
+    high[wide : wide + edge, :] = jnp.where(place[0] == line - 1, 0.0, after)
     high[0:wide, :] = tiles[z.rows - edge - wide : z.rows - edge, :]
     columns = flux_columns(z, matrix)
     for n in range(HALO):
@@ -557,7 +566,7 @@
             out_specs=[VM] * 3,
             scratch_shapes=[
                 pltpu.VMEM((blocks * SUB, LANES), I32),
-                pltpu.VMEM((LANES, LANES), F32),
+                pltpu.VMEM((SLOTS * LANES, LANES), F32),
                 *[pltpu.SMEM((SUB, LANES), I32) for _ in range(SLOTS)],
                 pltpu.SemaphoreType.DMA((SLOTS,)),
             ],
@@ -565,7 +574,7 @@
             name="receivers",
         )(place, receive, inbound, tiles)
         same_chip = lax.ppermute(same_chip, "line", [(i, i ^ 1) for i in range(count)])
-        facing = [(i, i + 1) for i in range(1, count - 1, 2)]
+        facing = [(i, (i + 1) % count) for i in range(1, count, 2)]
         next_chip = lax.ppermute(next_chip, "line", facing + [(b, a) for a, b in facing])
         layers = z.cl - 2 * HALO
         inner = pl.pallas_call(
@@ -581,7 +590,7 @@
             name="interior",
         )(tiles, start, speed_xi, speed_eta, matrix)
         outer, ends = pl.pallas_call(
-            functools.partial(edges_kernel, z),
+            functools.partial(edges_kernel, z, count),
             out_shape=[f32(2 * HALO * z.layer, LANES), f32(z.halves * s_rows, LANES)],
             in_specs=[SM] + [VM] * 13,
             out_specs=[VM] * 2,

time: 117 us -> 115 us (0.983)
  starting transfers between devices: 25.9 us -> 17.8 us
  waiting for transfers between devices: 23.4 us -> 29 us
    ppermute x9, starting transfers between devices: 10 us -> 1.72 us  [to_other_core(): lax.ppermute(array, 'line', [(i, i ^ 1) for i in range(lax.axis_size('lin...]
    ppermute x2, waiting for transfers between devices: 0.01 us -> 7.68 us  [local(): lax.ppermute(next_chip, 'line', facing + [(b, a) for a, b in facing])]
    ppermute x6, waiting for transfers between devices: 11 us -> 9.54 us  [from_other_chips(): there = lax.ppermute(array, 'line', [(i, i ^ 2 * s) for i in range(size)])]
  transfers between devices with their start and end apart: 20 -> 20, of which waited for: 13 -> 14; matrix products, arithmetic and copies ran while one was open for 0% -> 0% of each run, Pallas kernels for 3% -> 4%
where the time goes in v2:
time: 115 us; the launch traced here: 114 us
  Pallas kernels  54.2 us (47%)
  waiting for transfers between devices  29 us (25%)
  starting transfers between devices  17.8 us (15%)
  blocking collectives  9.19 us (8%)
  local copies, waits for them, and re-layouts  3.79 us (3%)
    pallas_call x1, Pallas kernels, local(): pl.pallas_call(functools.partial(solve_kernel, z, chips, False), out_shap...  16.3 us
    pallas_call x1, Pallas kernels, local(): pl.pallas_call(functools.partial(first_kernel, z), out_shape=[picked, til...  15.1 us
    pallas_call x2, Pallas kernels, local(): pl.pallas_call(functools.partial(place_kernel, z), out_shape=[tile_shape,...  11 us
    ppermute x6, waiting for transfers between devices, from_other_chips(): there = lax.ppermute(array, 'line', [(i, i ^ 2 * s) for i in range(size)])  9.54 us
    all_to_all x1, blocking collectives, local(): lax.all_to_all(values.reshape(devices, 4, LANES), ('line', 'batch'), 0, 0...  9.19 us
    ppermute x2, waiting for transfers between devices, local(): lax.ppermute(next_chip, 'line', facing + [(b, a) for a, b in facing])  7.68 us
    all_to_all x1, waiting for transfers between devices, local(): lax.all_to_all(values.reshape(devices, 4, LANES), ('line', 'batch'), 0, 0...  7.41 us
    all_to_all x1, starting transfers between devices, local(): lax.all_to_all(values.reshape(devices, 4, LANES), ('line', 'batch'), 0, 0...  7.32 us
  transfers between devices with their start and end apart: 20, of which 14 were waited for; matrix products, arithmetic and copies ran while one was open for 0% of the time, Pallas kernels for 4%

profile of v2, /device:TPU:0, one launch (start us, length us, event | category | flops | bytes accessed | tf_op | source)
XLA Modules:
  0.0 114.4 jit_solution(214604265528134018)
XLA Ops:
  0.0 1.3 %copy-done.7 = f32[6,24,8,256]{3,2,1,0:T(8,128)S(1)} copy-done((f32[6,24,8,256]{3,2,1,0:T(8,128)S(1)}, f32[6,24,8,256]{3,2,1,0:T(8,128)}, u32[]{:S(2)}) %copy-start.7) | copy-done | bytes 1179672
  1.3 0.8 copy-done.13
  2.2 0.8 copy-done.15
  3.0 15.1 %donors.1 = (f32[128,128]{1,0:T(8,128)}, f32[3584,128]{1,0:T(8,128)S(1)}) custom-call(s32[8,2048]{1,0:T(8,128)S(1)} %copy-done.13, f32[8,2048]{1,0:T(8,128)S(1)} %copy-done.15, f32[6,24,8,256]{3,2,1,0:T(8,128)S(1)} %copy-done.7), custom_call_target="tpu_custom_call" | custom-call | tf_op jit(solution)/shard_map/donors/pallas_call | solution.py:547
  18.1 7.3 %all-to-all-start = ((f32[32,4,128]{2,1,0:T(4,128)}), f32[32,4,128]{2,1,0:T(4,128)S(1)}, u32[]{:S(2)}, u32[]{:S(2)}) async-start(f32[32,4,128]{2,1,0:T(4,128)} %bitcast.4), calls=%async_computation | async-start | bytes 131072 | tf_op jit(solution)/shard_map/all_to_all | solution.py:560
  25.5 7.4 %all-to-all-done = f32[32,4,128]{2,1,0:T(4,128)S(1)} async-done(((f32[32,4,128]{2,1,0:T(4,128)}), f32[32,4,128]{2,1,0:T(4,128)S(1)}, u32[]{:S(2)}, u32[]{:S(2)}) %all-to-all-start) | async-done | bytes 65568 | tf_op jit(solution)/shard_map/all_to_all | solution.py:560
  32.9 0.7 copy-done.17
  33.6 5.5 %receivers.2 = (f32[3584,128]{1,0:T(8,128)S(1)}, f32[256,128]{1,0:T(8,128)S(1)}, f32[256,128]{1,0:T(8,128)S(1)}) custom-call(s32[3]{0:T(128)S(1)} %pad_add_fusion.place.refs_0_, s32[16,128]{1,0:T(8,128)S(1)} %bitcast.11, f32[128,128]{1,0:T(8,128)S(1)} %bitcast.8, f32[3584,128]{1,0:T(8,128)S(1)} %get-tuple-element.25.tiles.start), custom_call_target="tpu_custom_call" | custom-call | tf_op jit(solution)/shard_map/receivers/pallas_call | solution.py:562
  39.2 0.7 collective-permute-start.1
  40.0 1.9 %interior.2.inner.refs_19_ = f32[2560,128]{1,0:T(8,128)S(1)} custom-call(f32[3584,128]{1,0:T(8,128)S(1)} %get-tuple-element.26.tiles.refs_21_, f32[3584,128]{1,0:T(8,128)S(1)} %get-tuple-element.25.tiles.start, f32[24,8,256]{2,1,0:T(8,128)S(1)} %copy-done.5, f32[24,8,256]{2,1,0:T(8,128)S(1)} %copy-done.6, f32[8,128]{1,0:T(8,128)S(1)} %pad.4.matrix), custom_call_target="tpu_custom_call" | custom-call | flops 13107200 | bytes 5242880 | tf_op jit(solution)/shard_map/interior/pallas_call | solution.py:580
  42.0 3.8 %collective-permute-done.1.next_chip = f32[256,128]{1,0:T(8,128)S(1)} collective-permute-done((f32[256,128]{1,0:T(8,128)S(1)}, f32[256,128]{1,0:T(8,128)S(1)}, u32[]{:S(2)}, u32[]{:S(2)}) %collective-permute-start.1) | collective-permute-done | bytes 131104 | tf_op jit(solution)/shard_map/ppermute | solution.py:578
  45.8 1.5 %edges.2 = (f32[512,128]{1,0:T(8,128)S(1)}, f32[384,128]{1,0:T(8,128)S(1)}) custom-call(s32[3]{0:T(128)S(1)} %pad_add_fusion.place.refs_0_, f32[3584,128]{1,0:T(8,128)S(1)} %get-tuple-element.26.tiles.refs_21_, f32[3584,128]{1,0:T(8,128)S(1)} %get-tuple-element.25.tiles.start, f32[256,128]{1,0:T(8,128)S(1)} %collective-permute-done.same_chip, ...), custom_call_target="tpu_custom_call" | custom-call | tf_op jit(solution)/shard_map/edges/pallas_call | solution.py:592
  48.2 0.9 collective-permute-done.3.other_maps.refs_4_
  49.2 0.6 compose.2
  50.4 0.7 collective-permute-start.6
  51.1 2.3 %collective-permute-start.4 = (f32[288,128]{1,0:T(8,128)S(1)}, f32[288,128]{1,0:T(8,128)S(1)}, u32[]{:S(2)}, u32[]{:S(2)}) collective-permute-start(f32[288,128]{1,0:T(8,128)S(1)} %get-tuple-element.32), channel_id=1, source_target_pairs={{0,8},{4,12},{8,0},{12,4},{16,24},{20,28},{24,16},{28,20},{1,9},{5... | collective-permute-start | bytes 442376 | tf_op jit(solution)/shard_map/ppermute | solution.py:506
  53.4 4.1 %collective-permute-done.8.refs_11_.refs_17_ = f32[288,128]{1,0:T(8,128)S(1)} collective-permute-done((f32[288,128]{1,0:T(8,128)S(1)}, f32[288,128]{1,0:T(8,128)S(1)}, u32[]{:S(2)}, u32[]{:S(2)}) %collective-permute-start.8) | collective-permute-done | bytes 147488 | tf_op jit(solution)/shard_map/ppermute | solution.py:506
  57.5 1.7 %collective-permute-done.6.refs_9_.refs_15_ = f32[288,128]{1,0:T(8,128)S(1)} collective-permute-done((f32[288,128]{1,0:T(8,128)S(1)}, f32[288,128]{1,0:T(8,128)S(1)}, u32[]{:S(2)}, u32[]{:S(2)}) %collective-permute-start.6) | collective-permute-done | bytes 147488 | tf_op jit(solution)/shard_map/ppermute | solution.py:506
  59.8 0.9 collective-permute-done.7.refs_10_.refs_16_
  60.9 16.3 %solve_donors.1 = (f32[128,128]{1,0:T(8,128)S(1)}, f32[3584,128]{1,0:T(8,128)S(1)}) custom-call(s32[3]{0:T(128)S(1)} %pad_add_fusion.place.refs_0_, f32[384,128]{1,0:T(8,128)S(1)} %get-tuple-element.29.own.refs_1_, f32[384,128]{1,0:T(8,128)S(1)} %collective-permute-done.2.other.refs_2_, f32[192,128]{1,0:T(8,128)S(1)} %segments.1.own_maps.refs_3_, ...), custom_call_target="tpu_custom_call" | custom-call | tf_op jit(solution)/shard_map/solve_donors/pallas_call | solution.py:645
  77.2 9.2 %all_to_all.10 = f32[32,4,128]{2,1,0:T(4,128)S(1)} all-to-all(f32[32,4,128]{2,1,0:T(4,128)S(1)} %bitcast.10), channel_id=1, replica_groups=mesh['line'=8,'batch'=4] {'line','batch'}, dimensions={0} | all-to-all | bytes 131072 | tf_op jit(solution)/shard_map/all_to_all | solution.py:560
  86.4 5.5 %receivers.3 = (f32[3584,128]{1,0:T(8,128)S(1)}, f32[256,128]{1,0:T(8,128)S(1)}, f32[256,128]{1,0:T(8,128)S(1)}) custom-call(s32[3]{0:T(128)S(1)} %pad_add_fusion.place.refs_0_, s32[16,128]{1,0:T(8,128)S(1)} %bitcast.12, f32[128,128]{1,0:T(8,128)S(1)} %bitcast.9, f32[3584,128]{1,0:T(8,128)S(1)} %get-tuple-element.35.tiles), custom_call_target="tpu_custom_call" | custom-call | tf_op jit(solution)/shard_map/receivers/pallas_call | solution.py:562
  92.0 0.7 collective-permute-start.11
  92.7 1.9 %interior.3.inner.refs_19_ = f32[2560,128]{1,0:T(8,128)S(1)} custom-call(f32[3584,128]{1,0:T(8,128)S(1)} %get-tuple-element.36.tiles.refs_21_, f32[3584,128]{1,0:T(8,128)S(1)} %get-tuple-element.25.tiles.start, f32[24,8,256]{2,1,0:T(8,128)S(1)} %copy-done.5, f32[24,8,256]{2,1,0:T(8,128)S(1)} %copy-done.6, f32[8,128]{1,0:T(8,128)S(1)} %pad.4.matrix), custom_call_target="tpu_custom_call" | custom-call | flops 13107200 | bytes 5242880 | tf_op jit(solution)/shard_map/interior/pallas_call | solution.py:580
  94.6 3.9 %collective-permute-done.11.next_chip = f32[256,128]{1,0:T(8,128)S(1)} collective-permute-done((f32[256,128]{1,0:T(8,128)S(1)}, f32[256,128]{1,0:T(8,128)S(1)}, u32[]{:S(2)}, u32[]{:S(2)}) %collective-permute-start.11) | collective-permute-done | bytes 131104 | tf_op jit(solution)/shard_map/ppermute | solution.py:578
  98.6 1.6 %edges.3 = (f32[512,128]{1,0:T(8,128)S(1)}, f32[384,128]{1,0:T(8,128)S(1)}) custom-call(s32[3]{0:T(128)S(1)} %pad_add_fusion.place.refs_0_, f32[3584,128]{1,0:T(8,128)S(1)} %get-tuple-element.36.tiles.refs_21_, f32[3584,128]{1,0:T(8,128)S(1)} %get-tuple-element.25.tiles.start, f32[256,128]{1,0:T(8,128)S(1)} %collective-permute-done.10.same_chip, ...), custom_call_target="tpu_custom_call" | custom-call | tf_op jit(solution)/shard_map/edges/pallas_call | solution.py:592
  100.2 1.4 %collective-permute-done.12.other.refs_2_ = f32[384,128]{1,0:T(8,128)S(1)} collective-permute-done((f32[384,128]{1,0:T(8,128)S(1)}, f32[384,128]{1,0:T(8,128)S(1)}, u32[]{:S(2)}, u32[]{:S(2)}) %collective-permute-start.12) | collective-permute-done | bytes 196640 | tf_op jit(solution)/shard_map/ppermute | solution.py:499
  101.7 0.6 compose.3
  102.6 0.7 collective-permute-start.15
  103.3 2.5 %collective-permute-start.13 = (f32[192,128]{1,0:T(8,128)S(1)}, f32[192,128]{1,0:T(8,128)S(1)}, u32[]{:S(2)}, u32[]{:S(2)}) collective-permute-start(f32[192,128]{1,0:T(8,128)S(1)} %get-tuple-element.41), channel_id=1, source_target_pairs={{0,8},{4,12},{8,0},{12,4},{16,24},{20,28},{24,16},{28,20},{1,9},{5... | collective-permute-start | bytes 294920 | tf_op jit(solution)/shard_map/ppermute | solution.py:506
  105.8 3.1 %collective-permute-done.17.refs_11_ = f32[192,128]{1,0:T(8,128)S(1)} collective-permute-done((f32[192,128]{1,0:T(8,128)S(1)}, f32[192,128]{1,0:T(8,128)S(1)}, u32[]{:S(2)}, u32[]{:S(2)}) %collective-permute-start.17) | collective-permute-done | bytes 98336 | tf_op jit(solution)/shard_map/ppermute | solution.py:506
  111.0 3.4 %solve_last.1 = f32[6,24,8,256]{3,2,1,0:T(8,128)} custom-call(s32[3]{0:T(128)S(1)} %pad_add_fusion.place.refs_0_, f32[384,128]{1,0:T(8,128)S(1)} %get-tuple-element.39.own.refs_1_, f32[384,128]{1,0:T(8,128)S(1)} %collective-permute-done.12.other.refs_2_, f32[192,128]{1,0:T(8,128)S(1)} %segments.1.own_maps.refs_3_, ...), custom_call_target="tpu_custom_call" | custom-call | tf_op jit(solution)/shard_map/solve_last/pallas_call | solution.py:635
  (63 shorter events, 5.0 us)
Async XLA Ops:
  0.0 40.0 %copy-start.6 = (f32[24,8,256]{2,1,0:T(8,128)S(1)}, f32[24,8,256]{2,1,0:T(8,128)}, u32[]{:S(2)}) copy-start(f32[24,8,256]{2,1,0:T(8,128)} %speed_eta.7) | copy-start | bytes 589828
  0.0 40.0 %copy-start.5 = (f32[24,8,256]{2,1,0:T(8,128)S(1)}, f32[24,8,256]{2,1,0:T(8,128)}, u32[]{:S(2)}) copy-start(f32[24,8,256]{2,1,0:T(8,128)} %speed_xi.7) | copy-start | bytes 589828
  3.0 36.9 %copy-start.19 = (f32[6,6]{1,0:T(8,128)S(1)}, f32[6,6]{1,0:T(8,128)}, u32[]{:S(2)}) copy-start(f32[6,6]{1,0:T(8,128)} %param.18) | copy-start | bytes 436
  18.1 14.8 %all-to-all-start = ((f32[32,4,128]{2,1,0:T(4,128)}), f32[32,4,128]{2,1,0:T(4,128)S(1)}, u32[]{:S(2)}, u32[]{:S(2)}) async-start(f32[32,4,128]{2,1,0:T(4,128)} %bitcast.4), calls=%async_computation | async-start | bytes 131072 | tf_op jit(solution)/shard_map/all_to_all | solution.py:560
  39.1 2.9 %collective-permute-start = (f32[256,128]{1,0:T(8,128)S(1)}, f32[256,128]{1,0:T(8,128)S(1)}, u32[]{:S(2)}, u32[]{:S(2)}) collective-permute-start(f32[256,128]{1,0:T(8,128)S(1)} %get-tuple-element.27), channel_id=1, source_target_pairs={{0,4},{4,0},{8,12},{12,8},{16,20},{20,16},{24,28},{28,24},{1,5},{5... | collective-permute-start | bytes 393224 | tf_op jit(solution)/shard_map/ppermute | solution.py:576
  39.2 6.6 %collective-permute-start.1 = (f32[256,128]{1,0:T(8,128)S(1)}, f32[256,128]{1,0:T(8,128)S(1)}, u32[]{:S(2)}, u32[]{:S(2)}) collective-permute-start(f32[256,128]{1,0:T(8,128)S(1)} %get-tuple-element.28), channel_id=1, source_target_pairs={{4,8},{12,16},{20,24},{28,0},{8,4},{16,12},{24,20},{0,28},{5,9},{1... | collective-permute-start | bytes 393224 | tf_op jit(solution)/shard_map/ppermute | solution.py:578
  40.0 5.8 %copy-start = (f32[24,8,256]{2,1,0:T(8,128)S(1)}, f32[24,8,256]{2,1,0:T(8,128)}, u32[]{:S(2)}) copy-start(f32[24,8,256]{2,1,0:T(8,128)} %refs_22_.3) | copy-start | bytes 589828
  42.0 18.9 %copy-start.8 = (f32[24,8,256]{2,1,0:T(8,128)S(1)}, f32[24,8,256]{2,1,0:T(8,128)}, u32[]{:S(2)}) copy-start(f32[24,8,256]{2,1,0:T(8,128)} %refs_27_.3) | copy-start | bytes 589828
  42.0 18.9 %copy-start.9 = (f32[24,8,256]{2,1,0:T(8,128)S(1)}, f32[24,8,256]{2,1,0:T(8,128)}, u32[]{:S(2)}) copy-start(f32[24,8,256]{2,1,0:T(8,128)} %refs_28_.3) | copy-start | bytes 589828
  42.0 18.8 %copy-start.10 = (f32[24,8,256]{2,1,0:T(8,128)S(1)}, f32[24,8,256]{2,1,0:T(8,128)}, u32[]{:S(2)}) copy-start(f32[24,8,256]{2,1,0:T(8,128)} %refs_29_.3) | copy-start | bytes 589828
  42.0 18.8 %copy-start.11 = (f32[24,8,256]{2,1,0:T(8,128)S(1)}, f32[24,8,256]{2,1,0:T(8,128)}, u32[]{:S(2)}) copy-start(f32[24,8,256]{2,1,0:T(8,128)} %refs_30_.3) | copy-start | bytes 589828
  42.0 18.8 %copy-start.12 = (f32[24,8,256]{2,1,0:T(8,128)S(1)}, f32[24,8,256]{2,1,0:T(8,128)}, u32[]{:S(2)}) copy-start(f32[24,8,256]{2,1,0:T(8,128)} %refs_31_.3) | copy-start | bytes 589828
  42.0 18.8 %copy-start.14 = (s32[8,2048]{1,0:T(8,128)S(1)}, s32[8,2048]{1,0:T(8,128)}, u32[]{:S(2)}) copy-start(s32[8,2048]{1,0:T(8,128)} %refs_32_.1) | copy-start | bytes 196612
  42.0 18.8 %copy-start.16 = (f32[8,2048]{1,0:T(8,128)S(1)}, f32[8,2048]{1,0:T(8,128)}, u32[]{:S(2)}) copy-start(f32[8,2048]{1,0:T(8,128)} %refs_33_.1) | copy-start | bytes 196612
  47.4 1.8 %collective-permute-start.2 = (f32[384,128]{1,0:T(8,128)S(1)}, f32[384,128]{1,0:T(8,128)S(1)}, u32[]{:S(2)}, u32[]{:S(2)}) collective-permute-start(f32[384,128]{1,0:T(8,128)S(1)} %get-tuple-element.29.own.refs_1_), channel_id=1, source_target_pairs={{0,4},{4,0},{8,12},{12,8},{16,20},{20,16},{24,28},{28,24},{1,5},{5... | collective-permute-start | bytes 589832 | tf_op jit(solution)/shard_map/ppermute | solution.py:499
  47.7 1.5 %collective-permute-start.3 = (f32[192,128]{1,0:T(8,128)S(1)}, f32[192,128]{1,0:T(8,128)S(1)}, u32[]{:S(2)}, u32[]{:S(2)}) collective-permute-start(f32[192,128]{1,0:T(8,128)S(1)} %segments.1.own_maps.refs_3_), channel_id=1, source_target_pairs={{0,4},{4,0},{8,12},{12,8},{16,20},{20,16},{24,28},{28,24},{1,5},{5... | collective-permute-start | bytes 294920 | tf_op jit(solution)/shard_map/ppermute | solution.py:499
  49.8 7.7 %collective-permute-start.8 = (f32[288,128]{1,0:T(8,128)S(1)}, f32[288,128]{1,0:T(8,128)S(1)}, u32[]{:S(2)}, u32[]{:S(2)}) collective-permute-start(f32[288,128]{1,0:T(8,128)S(1)} %get-tuple-element.32), channel_id=1, source_target_pairs={{0,24},{4,28},{8,16},{12,20},{16,8},{20,12},{24,0},{28,4},{1,25},{... | collective-permute-start | bytes 442376 | tf_op jit(solution)/shard_map/ppermute | solution.py:506
  50.4 8.8 %collective-permute-start.6 = (f32[288,128]{1,0:T(8,128)S(1)}, f32[288,128]{1,0:T(8,128)S(1)}, u32[]{:S(2)}, u32[]{:S(2)}) collective-permute-start(f32[288,128]{1,0:T(8,128)S(1)} %get-tuple-element.32), channel_id=1, source_target_pairs={{0,16},{4,20},{8,24},{12,28},{16,0},{20,4},{24,8},{28,12},{1,17},{... | collective-permute-start | bytes 442376 | tf_op jit(solution)/shard_map/ppermute | solution.py:506
  51.1 8.2 %collective-permute-start.4 = (f32[288,128]{1,0:T(8,128)S(1)}, f32[288,128]{1,0:T(8,128)S(1)}, u32[]{:S(2)}, u32[]{:S(2)}) collective-permute-start(f32[288,128]{1,0:T(8,128)S(1)} %get-tuple-element.32), channel_id=1, source_target_pairs={{0,8},{4,12},{8,0},{12,4},{16,24},{20,28},{24,16},{28,20},{1,9},{5... | collective-permute-start | bytes 442376 | tf_op jit(solution)/shard_map/ppermute | solution.py:506
  57.5 2.2 %collective-permute-start.9 = (f32[288,128]{1,0:T(8,128)S(1)}, f32[288,128]{1,0:T(8,128)S(1)}, u32[]{:S(2)}, u32[]{:S(2)}) collective-permute-start(f32[288,128]{1,0:T(8,128)S(1)} %collective-permute-done.8.refs_11_.refs_17_), channel_id=1, source_target_pairs={{0,4},{4,0},{8,12},{12,8},{16,20},{20,16},{24,28},{28,24},{1,5},{5... | collective-permute-start | bytes 442376 | tf_op jit(solution)/shard_map/ppermute | solution.py:499
  59.2 1.4 %collective-permute-start.7 = (f32[288,128]{1,0:T(8,128)S(1)}, f32[288,128]{1,0:T(8,128)S(1)}, u32[]{:S(2)}, u32[]{:S(2)}) collective-permute-start(f32[288,128]{1,0:T(8,128)S(1)} %collective-permute-done.6.refs_9_.refs_15_), channel_id=1, source_target_pairs={{0,4},{4,0},{8,12},{12,8},{16,20},{20,16},{24,28},{28,24},{1,5},{5... | collective-permute-start | bytes 442376 | tf_op jit(solution)/shard_map/ppermute | solution.py:499
  59.2 1.6 %collective-permute-start.5 = (f32[288,128]{1,0:T(8,128)S(1)}, f32[288,128]{1,0:T(8,128)S(1)}, u32[]{:S(2)}, u32[]{:S(2)}) collective-permute-start(f32[288,128]{1,0:T(8,128)S(1)} %collective-permute-done.4.refs_7_.refs_13_), channel_id=1, source_target_pairs={{0,4},{4,0},{8,12},{12,8},{16,20},{20,16},{24,28},{28,24},{1,5},{5... | collective-permute-start | bytes 442376 | tf_op jit(solution)/shard_map/ppermute | solution.py:499
  60.9 25.5 %copy-start.18 = (s32[2048]{0:T(1024)S(1)}, s32[2048]{0:T(1024)}, u32[]{:S(2)}) copy-start(s32[2048]{0:T(1024)} %param.33) | copy-start | bytes 24580
  91.9 2.7 %collective-permute-start.10 = (f32[256,128]{1,0:T(8,128)S(1)}, f32[256,128]{1,0:T(8,128)S(1)}, u32[]{:S(2)}, u32[]{:S(2)}) collective-permute-start(f32[256,128]{1,0:T(8,128)S(1)} %get-tuple-element.37), channel_id=1, source_target_pairs={{0,4},{4,0},{8,12},{12,8},{16,20},{20,16},{24,28},{28,24},{1,5},{5... | collective-permute-start | bytes 393224 | tf_op jit(solution)/shard_map/ppermute | solution.py:576
  92.0 6.6 %collective-permute-start.11 = (f32[256,128]{1,0:T(8,128)S(1)}, f32[256,128]{1,0:T(8,128)S(1)}, u32[]{:S(2)}, u32[]{:S(2)}) collective-permute-start(f32[256,128]{1,0:T(8,128)S(1)} %get-tuple-element.38), channel_id=1, source_target_pairs={{4,8},{12,16},{20,24},{28,0},{8,4},{16,12},{24,20},{0,28},{5,9},{1... | collective-permute-start | bytes 393224 | tf_op jit(solution)/shard_map/ppermute | solution.py:578
  100.1 1.5 %collective-permute-start.12 = (f32[384,128]{1,0:T(8,128)S(1)}, f32[384,128]{1,0:T(8,128)S(1)}, u32[]{:S(2)}, u32[]{:S(2)}) collective-permute-start(f32[384,128]{1,0:T(8,128)S(1)} %get-tuple-element.39.own.refs_1_), channel_id=1, source_target_pairs={{0,4},{4,0},{8,12},{12,8},{16,20},{20,16},{24,28},{28,24},{1,5},{5... | collective-permute-start | bytes 589832 | tf_op jit(solution)/shard_map/ppermute | solution.py:499
  102.3 6.7 %collective-permute-start.17 = (f32[192,128]{1,0:T(8,128)S(1)}, f32[192,128]{1,0:T(8,128)S(1)}, u32[]{:S(2)}, u32[]{:S(2)}) collective-permute-start(f32[192,128]{1,0:T(8,128)S(1)} %get-tuple-element.41), channel_id=1, source_target_pairs={{0,24},{4,28},{8,16},{12,20},{16,8},{20,12},{24,0},{28,4},{1,25},{... | collective-permute-start | bytes 294920 | tf_op jit(solution)/shard_map/ppermute | solution.py:506
  102.6 6.9 %collective-permute-start.15 = (f32[192,128]{1,0:T(8,128)S(1)}, f32[192,128]{1,0:T(8,128)S(1)}, u32[]{:S(2)}, u32[]{:S(2)}) collective-permute-start(f32[192,128]{1,0:T(8,128)S(1)} %get-tuple-element.41), channel_id=1, source_target_pairs={{0,16},{4,20},{8,24},{12,28},{16,0},{20,4},{24,8},{28,12},{1,17},{... | collective-permute-start | bytes 294920 | tf_op jit(solution)/shard_map/ppermute | solution.py:506
  103.3 6.2 %collective-permute-start.13 = (f32[192,128]{1,0:T(8,128)S(1)}, f32[192,128]{1,0:T(8,128)S(1)}, u32[]{:S(2)}, u32[]{:S(2)}) collective-permute-start(f32[192,128]{1,0:T(8,128)S(1)} %get-tuple-element.41), channel_id=1, source_target_pairs={{0,8},{4,12},{8,0},{12,4},{16,24},{20,28},{24,16},{28,20},{1,9},{5... | collective-permute-start | bytes 294920 | tf_op jit(solution)/shard_map/ppermute | solution.py:506
  108.9 1.3 %collective-permute-start.18 = (f32[192,128]{1,0:T(8,128)S(1)}, f32[192,128]{1,0:T(8,128)S(1)}, u32[]{:S(2)}, u32[]{:S(2)}) collective-permute-start(f32[192,128]{1,0:T(8,128)S(1)} %collective-permute-done.17.refs_11_), channel_id=1, source_target_pairs={{0,4},{4,0},{8,12},{12,8},{16,20},{20,16},{24,28},{28,24},{1,5},{5... | collective-permute-start | bytes 294920 | tf_op jit(solution)/shard_map/ppermute | solution.py:499
  109.5 1.3 %collective-permute-start.16 = (f32[192,128]{1,0:T(8,128)S(1)}, f32[192,128]{1,0:T(8,128)S(1)}, u32[]{:S(2)}, u32[]{:S(2)}) collective-permute-start(f32[192,128]{1,0:T(8,128)S(1)} %collective-permute-done.15.refs_9_), channel_id=1, source_target_pairs={{0,4},{4,0},{8,12},{12,8},{16,20},{20,16},{24,28},{28,24},{1,5},{5... | collective-permute-start | bytes 294920 | tf_op jit(solution)/shard_map/ppermute | solution.py:499
  109.5 1.5 %collective-permute-start.14 = (f32[192,128]{1,0:T(8,128)S(1)}, f32[192,128]{1,0:T(8,128)S(1)}, u32[]{:S(2)}, u32[]{:S(2)}) collective-permute-start(f32[192,128]{1,0:T(8,128)S(1)} %collective-permute-done.13.refs_7_), channel_id=1, source_target_pairs={{0,4},{4,0},{8,12},{12,8},{16,20},{20,16},{24,28},{28,24},{1,5},{5... | collective-permute-start | bytes 294920 | tf_op jit(solution)/shard_map/ppermute | solution.py:499
  (8 other events, 27.0 us)
